TPU v7x, 32 devices: a whole 2x2x4 slice. The times are simulated.
32 devices in a mesh: seq: 2 (over x), shard: 16 (over z, y, core).
Axes of the slice: x: 2, y: 2, z: 4, core: 2. Of those that a mesh axis runs over, the one named last changes fastest.
Arguments:
- tokens: bfloat16 [16, 1024, 1024], P('shard', 'seq'), may hold values from -6 to 6
- doc_starts: int32 [16, 4], P('shard'), may hold values from 0 to 1023, as said below
- norm_gain: bfloat16 [1024], P('shard'), may hold values from 0.5 to 1.5
- query_weight: bfloat16 [1024, 1024], P('shard'), may hold values from -0.1875 to 0.1875
- key_weight: bfloat16 [1024, 1024], P('shard'), may hold values from -0.1875 to 0.1875
- value_weight: bfloat16 [1024, 2048], P('shard'), may hold values from -0.1875 to 0.1875
- gate_weight: bfloat16 [1024, 2048], P('shard'), may hold values from -0.1875 to 0.1875
- beta_decay_weight: bfloat16 [1024, 16], P('shard'), may hold values from -0.1875 to 0.1875
- conv_filters: float32 [4, 8, 512], P(None, 'seq'), may hold values from -2.5 to 2.5
- decay_params: float32 [8, 2], P('seq'), may hold values from -10 to 2.5
- out_norm_gain: bfloat16 [256], P('shard'), may hold values from 0.5 to 1.5
- out_weight: bfloat16 [2048, 1024], P('shard'), may hold values from -0.125 to 0.125
- ffn_norm_gain: bfloat16 [1024], P('shard'), may hold values from 0.5 to 1.5
- ffn_gate_weight: bfloat16 [1024, 2816], P('shard'), may hold values from -0.1875 to 0.1875
- ffn_up_weight: bfloat16 [1024, 2816], P('shard'), may hold values from -0.1875 to 0.1875
- down_weight: bfloat16 [2816, 1024], P('shard'), may hold values from -0.109375 to 0.109375
- out_cotangent: bfloat16 [16, 1024, 1024], P('shard', 'seq'), may hold values from -6 to 6
Outputs:
- block_out: bfloat16 [16, 1024, 1024], P('shard', 'seq')
- tokens_grad: float32 [16, 1024, 1024], P('shard', 'seq')
- norm_gain_grad: float32 [1024], P('shard')
- query_weight_grad: float32 [1024, 1024], P('shard')
- key_weight_grad: float32 [1024, 1024], P('shard')
- value_weight_grad: float32 [1024, 2048], P('shard')
- gate_weight_grad: float32 [1024, 2048], P('shard')
- beta_decay_weight_grad: float32 [1024, 16], P('shard')
- conv_filters_grad: float32 [4, 8, 512], P(None, 'seq')
- decay_params_grad: float32 [8, 2], P('seq')
- out_norm_gain_grad: float32 [256], P('shard')
- out_weight_grad: float32 [2048, 1024], P('shard')
- ffn_norm_gain_grad: float32 [1024], P('shard')
- ffn_gate_weight_grad: float32 [1024, 2816], P('shard')
- ffn_up_weight_grad: float32 [1024, 2816], P('shard')
- down_weight_grad: float32 [2816, 1024], P('shard')
Inputs may be any that keep to these rules, and one draw needn't show every extreme that they name: `doc_starts`: each row holds 4 document start positions in strictly increasing order, the first of which is 0.
All inputs are finite; a program needn't handle non-finite values.
Results may differ from a plain program's by a relative error of at most 0.022.
Values may be sent and summed in bfloat16 or wider, within the bound.
No kernel may reach another device: no remote copies, remote signals or barrier semaphores. Data moves between devices by JAX's collectives and lax.ppermute only.
A program may use at most 320 MiB of HBM per device.

v0:
```python
import jax
import jax.numpy as jnp
from jax import lax
from jax.sharding import PartitionSpec as P

HEADS = 8
KEY = 128
VALUE = 256
CONV = 4
GROUP = 64


epsilon = 1e-06
highest = lax.Precision.HIGHEST


def product(left_side, right_side):
    return jnp.dot(left_side, right_side, precision=highest, preferred_element_type=jnp.float32)


def forward_dot(left_side, right_side):
    return jnp.dot(left_side, right_side, preferred_element_type=jnp.float32)


def times_transposed(left_side, right_side):
    return lax.dot_general(
        left_side, right_side, (((1,), (1,)), ((), ())), preferred_element_type=jnp.float32
    )


def transposed_times(left_side, right_side):
    return lax.dot_general(
        left_side, right_side, (((0,), (0,)), ((), ())), preferred_element_type=jnp.float32
    )


def rms_norm(values, gain):
    return values * lax.rsqrt(jnp.mean(values * values, axis=-1, keepdims=True) + epsilon) * gain


def gated_norm(values, gates, gain):
    return rms_norm(values, gain) * jax.nn.silu(gates)


def swiglu(gate_rows, up_rows):
    return jax.nn.silu(gate_rows) * up_rows


def document_ids(starts, length):
    places = lax.broadcasted_iota(jnp.int32, (length, starts.shape[0]), 0)
    return jnp.sum((places >= starts[None, :]).astype(jnp.int32), axis=1) - 1


def causal_conv(inputs, filters, doc_ids):
    length, channels = inputs.shape
    summed = inputs * filters[CONV - 1]
    for offset in range(1, CONV):
        shifted = jnp.concatenate(
            [jnp.zeros((offset, channels), jnp.float32), inputs[: length - offset]], axis=0
        )
        shifted_docs = jnp.concatenate(
            [jnp.full((offset,), -1, jnp.int32), doc_ids[: length - offset]]
        )
        same_doc = (shifted_docs == doc_ids).astype(jnp.float32)
        summed = summed + shifted * same_doc[:, None] * filters[CONV - 1 - offset]
    return jax.nn.silu(summed)


def delta_rule(query_rows, key_rows, value_rows, strength, log_decay, doc_ids):
    length, key_width = key_rows.shape
    value_width = value_rows.shape[1]
    blocks = length // GROUP
    query_blocks = query_rows.reshape(blocks, GROUP, key_width)
    key_blocks = key_rows.reshape(blocks, GROUP, key_width)
    value_blocks = value_rows.reshape(blocks, GROUP, value_width)
    beta_blocks = strength.reshape(blocks, GROUP)
    decay_sums = jnp.cumsum(log_decay.reshape(blocks, GROUP), axis=1)
    doc_blocks = doc_ids.reshape(blocks, GROUP)
    previous = jnp.concatenate(
        [jnp.full((1,), -1, jnp.int32), doc_ids[GROUP - 1 : length - 1 : GROUP]]
    )
    carried = (doc_blocks == previous[:, None]).astype(jnp.float32)
    same_doc = doc_blocks[:, :, None] == doc_blocks[:, None, :]
    row_index = lax.broadcasted_iota(jnp.int32, (GROUP, GROUP), 0)
    column_index = lax.broadcasted_iota(jnp.int32, (GROUP, GROUP), 1)
    strictly = same_doc & (row_index > column_index)[None]
    inclusive = same_doc & (row_index >= column_index)[None]
    decay_gap = decay_sums[:, :, None] - decay_sums[:, None, :]
    fade_lower = jnp.where(strictly, jnp.exp(jnp.where(strictly, decay_gap, 0.0)), 0.0)
    fade_upper = jnp.where(inclusive, jnp.exp(jnp.where(inclusive, decay_gap, 0.0)), 0.0)
    key_gram = jnp.einsum("cik,cjk->cij", key_blocks, key_blocks, precision=highest)
    system = (
        jnp.eye(GROUP, dtype=jnp.float32)[None] + beta_blocks[:, :, None] * key_gram * fade_lower
    )
    entering = jnp.exp(decay_sums) * carried
    right_side = jnp.concatenate(
        [beta_blocks[:, :, None] * value_blocks, (beta_blocks * entering)[:, :, None] * key_blocks],
        axis=2,
    )
    solved = jax.scipy.linalg.solve_triangular(system, right_side, lower=True, unit_diagonal=True)
    new_values = solved[:, :, :value_width]
    corrections = solved[:, :, value_width:]
    scores = jnp.einsum("cik,cjk->cij", query_blocks, key_blocks, precision=highest) * fade_upper
    query_in = entering[:, :, None] * query_blocks
    same_last = doc_blocks == doc_blocks[:, -1:]
    fade_last = jnp.where(
        same_last, jnp.exp(jnp.where(same_last, decay_sums[:, -1:] - decay_sums, 0.0)), 0.0
    )
    key_out = fade_last[:, :, None] * key_blocks
    retain = entering[:, -1]

    def advance(memory, pieces):
        block_values, block_corr, block_scores, block_query, block_keys, block_retain = pieces
        deltas = block_values - product(block_corr, memory)
        outputs = product(block_query, memory) + product(block_scores, deltas)
        memory = block_retain * memory + product(block_keys.T, deltas)
        return (memory, outputs)

    start = jnp.zeros((key_width, value_width), jnp.float32)
    final_memory, outputs = lax.scan(
        jax.checkpoint(advance), start, (new_values, corrections, scores, query_in, key_out, retain)
    )
    return outputs.reshape(length, value_width)


def head_mixer(query_raw, key_raw, value_raw, logits, filters, decay_pair, doc_ids):
    key_width = query_raw.shape[1]
    convolved = causal_conv(
        jnp.concatenate([query_raw, key_raw, value_raw], axis=1), filters, doc_ids
    )
    query_rows = convolved[:, :key_width]
    key_rows = convolved[:, key_width : 2 * key_width]
    value_rows = convolved[:, 2 * key_width :]
    query_rows = (
        query_rows
        * lax.rsqrt(jnp.sum(query_rows * query_rows, axis=1, keepdims=True) + epsilon)
        * key_width ** (-0.5)
    )
    key_rows = key_rows * lax.rsqrt(jnp.sum(key_rows * key_rows, axis=1, keepdims=True) + epsilon)
    strength = jax.nn.sigmoid(logits[:, 0])
    log_decay = -jnp.exp(decay_pair[0]) * jax.nn.softplus(logits[:, 1] + decay_pair[1])
    return delta_rule(query_rows, key_rows, value_rows, strength, log_decay, doc_ids)


def on_device(
    tokens,
    doc_starts,
    norm_gain,
    query_weight,
    key_weight,
    value_weight,
    gate_weight,
    beta_decay_weight,
    conv_filters,
    decay_params,
    out_norm_gain,
    out_weight,
    ffn_norm_gain,
    ffn_gate_weight,
    ffn_up_weight,
    down_weight,
    out_cotangent,
):
    mixer_full = (
        lax.all_gather(norm_gain, "shard", axis=0, tiled=True),
        lax.all_gather(query_weight, "shard", axis=0, tiled=True),
        lax.all_gather(key_weight, "shard", axis=0, tiled=True),
        lax.all_gather(value_weight, "shard", axis=0, tiled=True),
        lax.all_gather(gate_weight, "shard", axis=0, tiled=True),
        lax.all_gather(beta_decay_weight, "shard", axis=0, tiled=True),
        lax.all_gather(out_norm_gain, "shard", axis=0, tiled=True),
        lax.all_gather(out_weight, "shard", axis=0, tiled=True),
    )
    ffn_full = (
        lax.all_gather(ffn_norm_gain, "shard", axis=0, tiled=True),
        lax.all_gather(ffn_gate_weight, "shard", axis=0, tiled=True),
        lax.all_gather(ffn_up_weight, "shard", axis=0, tiled=True),
        lax.all_gather(down_weight, "shard", axis=0, tiled=True),
    )
    inputs = tokens[0].astype(jnp.float32)
    token_count = inputs.shape[0]
    length = token_count * lax.axis_size("seq")
    doc_ids = document_ids(doc_starts[0], length)
    first_norm, first_pull = jax.vjp(rms_norm, inputs, mixer_full[0].astype(jnp.float32))
    normed = first_norm.astype(jnp.bfloat16)
    query_raw = forward_dot(normed, mixer_full[1]).astype(jnp.bfloat16)
    key_raw = forward_dot(normed, mixer_full[2]).astype(jnp.bfloat16)
    value_raw = forward_dot(normed, mixer_full[3]).astype(jnp.bfloat16)
    gate_rows = forward_dot(normed, mixer_full[4])
    logits = forward_dot(normed, mixer_full[5]).astype(jnp.bfloat16)
    heads_in = (
        lax.all_to_all(
            query_raw.reshape(token_count, HEADS, KEY),
            "seq",
            split_axis=1,
            concat_axis=0,
            tiled=True,
        ),
        lax.all_to_all(
            key_raw.reshape(token_count, HEADS, KEY), "seq", split_axis=1, concat_axis=0, tiled=True
        ),
        lax.all_to_all(
            value_raw.reshape(token_count, HEADS, VALUE),
            "seq",
            split_axis=1,
            concat_axis=0,
            tiled=True,
        ),
        lax.all_to_all(
            logits.reshape(token_count, HEADS, 2), "seq", split_axis=1, concat_axis=0, tiled=True
        ),
    )

    def local_mixer(query_in, key_in, value_in, logit_in, filters, decay_pair):
        mixer = jax.vmap(head_mixer, in_axes=(1, 1, 1, 1, 1, 0, None), out_axes=1)
        return mixer(query_in, key_in, value_in, logit_in, filters, decay_pair, doc_ids)

    mixed, mixer_pull = jax.vjp(
        local_mixer,
        heads_in[0].astype(jnp.float32),
        heads_in[1].astype(jnp.float32),
        heads_in[2].astype(jnp.float32),
        heads_in[3].astype(jnp.float32),
        conv_filters,
        decay_params,
    )
    returned = lax.all_to_all(
        mixed.astype(jnp.bfloat16), "seq", split_axis=0, concat_axis=1, tiled=True
    )
    gated, gated_pull = jax.vjp(
        gated_norm,
        returned.astype(jnp.float32),
        gate_rows.reshape(token_count, HEADS, VALUE),
        mixer_full[6].astype(jnp.float32),
    )
    gated_low = gated.reshape(token_count, HEADS * VALUE).astype(jnp.bfloat16)
    middle = inputs + forward_dot(gated_low, mixer_full[7])
    second_norm, second_pull = jax.vjp(rms_norm, middle, ffn_full[0].astype(jnp.float32))
    hidden = second_norm.astype(jnp.bfloat16)
    gate_ffn = forward_dot(hidden, ffn_full[1])
    up_ffn = forward_dot(hidden, ffn_full[2])
    activated, swiglu_pull = jax.vjp(swiglu, gate_ffn, up_ffn)
    activated_low = activated.astype(jnp.bfloat16)
    block_out = (middle + forward_dot(activated_low, ffn_full[3])).astype(jnp.bfloat16)
    mixer_back = (
        lax.all_gather(norm_gain, "shard", axis=0, tiled=True),
        lax.all_gather(query_weight, "shard", axis=0, tiled=True),
        lax.all_gather(key_weight, "shard", axis=0, tiled=True),
        lax.all_gather(value_weight, "shard", axis=0, tiled=True),
        lax.all_gather(gate_weight, "shard", axis=0, tiled=True),
        lax.all_gather(beta_decay_weight, "shard", axis=0, tiled=True),
        lax.all_gather(out_norm_gain, "shard", axis=0, tiled=True),
        lax.all_gather(out_weight, "shard", axis=0, tiled=True),
    )
    ffn_back = (
        lax.all_gather(ffn_norm_gain, "shard", axis=0, tiled=True),
        lax.all_gather(ffn_gate_weight, "shard", axis=0, tiled=True),
        lax.all_gather(ffn_up_weight, "shard", axis=0, tiled=True),
        lax.all_gather(down_weight, "shard", axis=0, tiled=True),
    )
    cotangent = out_cotangent[0]
    act_grad = times_transposed(cotangent, ffn_back[3])
    down_grad = transposed_times(activated_low, cotangent)
    gate_ffn_grad, up_ffn_grad = swiglu_pull(act_grad)
    gate_ffn_low = gate_ffn_grad.astype(jnp.bfloat16)
    up_ffn_low = up_ffn_grad.astype(jnp.bfloat16)
    ffn_gate_grad = transposed_times(hidden, gate_ffn_low)
    ffn_up_grad = transposed_times(hidden, up_ffn_low)
    hidden_grad = times_transposed(gate_ffn_low, ffn_back[1]) + times_transposed(
        up_ffn_low, ffn_back[2]
    )
    middle_part, ffn_gain_grad = second_pull(hidden_grad)
    middle_grad = cotangent.astype(jnp.float32) + middle_part
    branch_low = middle_grad.astype(jnp.bfloat16)
    out_grad = transposed_times(gated_low, branch_low)
    gated_grad = times_transposed(branch_low, mixer_back[7]).reshape(token_count, HEADS, VALUE)
    mixed_grad, gate_rows_grad, out_gain_grad = gated_pull(gated_grad)
    heads_grad = lax.all_to_all(
        mixed_grad.astype(jnp.bfloat16), "seq", split_axis=1, concat_axis=0, tiled=True
    )
    query_grad, key_grad, value_grad, logit_grad, filter_grad, decay_grad = mixer_pull(
        heads_grad.astype(jnp.float32)
    )
    tokens_back = (
        lax.all_to_all(
            query_grad.astype(jnp.bfloat16), "seq", split_axis=0, concat_axis=1, tiled=True
        ),
        lax.all_to_all(
            key_grad.astype(jnp.bfloat16), "seq", split_axis=0, concat_axis=1, tiled=True
        ),
        lax.all_to_all(
            value_grad.astype(jnp.bfloat16), "seq", split_axis=0, concat_axis=1, tiled=True
        ),
        lax.all_to_all(
            logit_grad.astype(jnp.bfloat16), "seq", split_axis=0, concat_axis=1, tiled=True
        ),
    )
    query_low = tokens_back[0].reshape(token_count, HEADS * KEY)
    key_low = tokens_back[1].reshape(token_count, HEADS * KEY)
    value_low = tokens_back[2].reshape(token_count, HEADS * VALUE)
    logit_low = tokens_back[3].reshape(token_count, HEADS * 2)
    gate_low = gate_rows_grad.reshape(token_count, HEADS * VALUE).astype(jnp.bfloat16)
    query_weight_grad = transposed_times(normed, query_low)
    key_weight_grad = transposed_times(normed, key_low)
    value_weight_grad = transposed_times(normed, value_low)
    gate_weight_grad = transposed_times(normed, gate_low)
    logit_weight_grad = transposed_times(normed, logit_low)
    normed_grad = (
        times_transposed(query_low, mixer_back[1])
        + times_transposed(key_low, mixer_back[2])
        + times_transposed(value_low, mixer_back[3])
        + times_transposed(gate_low, mixer_back[4])
        + times_transposed(logit_low, mixer_back[5])
    )
    input_part, norm_gain_grad = first_pull(normed_grad)
    tokens_grad = middle_grad + input_part
    shares = (
        lax.psum_scatter(
            norm_gain_grad.astype(jnp.bfloat16), "shard", scatter_dimension=0, tiled=True
        ).astype(jnp.float32),
        lax.psum_scatter(
            query_weight_grad.astype(jnp.bfloat16), "shard", scatter_dimension=0, tiled=True
        ).astype(jnp.float32),
        lax.psum_scatter(
            key_weight_grad.astype(jnp.bfloat16), "shard", scatter_dimension=0, tiled=True
        ).astype(jnp.float32),
        lax.psum_scatter(
            value_weight_grad.astype(jnp.bfloat16), "shard", scatter_dimension=0, tiled=True
        ).astype(jnp.float32),
        lax.psum_scatter(
            gate_weight_grad.astype(jnp.bfloat16), "shard", scatter_dimension=0, tiled=True
        ).astype(jnp.float32),
        lax.psum_scatter(
            logit_weight_grad.astype(jnp.bfloat16), "shard", scatter_dimension=0, tiled=True
        ).astype(jnp.float32),
        lax.psum_scatter(
            out_gain_grad.astype(jnp.bfloat16), "shard", scatter_dimension=0, tiled=True
        ).astype(jnp.float32),
        lax.psum_scatter(
            out_grad.astype(jnp.bfloat16), "shard", scatter_dimension=0, tiled=True
        ).astype(jnp.float32),
        lax.psum_scatter(
            ffn_gain_grad.astype(jnp.bfloat16), "shard", scatter_dimension=0, tiled=True
        ).astype(jnp.float32),
        lax.psum_scatter(
            ffn_gate_grad.astype(jnp.bfloat16), "shard", scatter_dimension=0, tiled=True
        ).astype(jnp.float32),
        lax.psum_scatter(
            ffn_up_grad.astype(jnp.bfloat16), "shard", scatter_dimension=0, tiled=True
        ).astype(jnp.float32),
        lax.psum_scatter(
            down_grad.astype(jnp.bfloat16), "shard", scatter_dimension=0, tiled=True
        ).astype(jnp.float32),
    )
    summed = (
        lax.psum(shares[0].astype(jnp.bfloat16), "seq").astype(jnp.float32),
        lax.psum(shares[1].astype(jnp.bfloat16), "seq").astype(jnp.float32),
        lax.psum(shares[2].astype(jnp.bfloat16), "seq").astype(jnp.float32),
        lax.psum(shares[3].astype(jnp.bfloat16), "seq").astype(jnp.float32),
        lax.psum(shares[4].astype(jnp.bfloat16), "seq").astype(jnp.float32),
        lax.psum(shares[5].astype(jnp.bfloat16), "seq").astype(jnp.float32),
        lax.psum(shares[6].astype(jnp.bfloat16), "seq").astype(jnp.float32),
        lax.psum(shares[7].astype(jnp.bfloat16), "seq").astype(jnp.float32),
        lax.psum(shares[8].astype(jnp.bfloat16), "seq").astype(jnp.float32),
        lax.psum(shares[9].astype(jnp.bfloat16), "seq").astype(jnp.float32),
        lax.psum(shares[10].astype(jnp.bfloat16), "seq").astype(jnp.float32),
        lax.psum(shares[11].astype(jnp.bfloat16), "seq").astype(jnp.float32),
    )
    head_sums = lax.psum((filter_grad, decay_grad), "shard")
    return (
        block_out[None],
        tokens_grad[None],
        summed[0],
        summed[1],
        summed[2],
        summed[3],
        summed[4],
        summed[5],
        head_sums[0],
        head_sums[1],
        summed[6],
        summed[7],
        summed[8],
        summed[9],
        summed[10],
        summed[11],
    )


def solution(mesh):
    in_specs = (
        P("shard", "seq", None),
        P("shard", None),
        P("shard"),
        P("shard", None),
        P("shard", None),
        P("shard", None),
        P("shard", None),
        P("shard", None),
        P(None, "seq", None),
        P("seq", None),
        P("shard"),
        P("shard", None),
        P("shard"),
        P("shard", None),
        P("shard", None),
        P("shard", None),
        P("shard", "seq", None),
    )
    out_specs = (
        P("shard", "seq", None),
        P("shard", "seq", None),
        P("shard"),
        P("shard", None),
        P("shard", None),
        P("shard", None),
        P("shard", None),
        P("shard", None),
        P(None, "seq", None),
        P("seq", None),
        P("shard"),
        P("shard", None),
        P("shard"),
        P("shard", None),
        P("shard", None),
        P("shard", None),
    )
    return jax.shard_map(
        on_device, mesh=mesh, in_specs=in_specs, out_specs=out_specs, check_vma=False
    )
```

profile of v0, /device:TPU:0, one launch (start us, length us, event | category | flops | bytes accessed | tf_op | source)
XLA Modules:
  0.0 2091.2 jit_solution(9120686903368685601)
XLA Ops:
  17.1 36.3 %all-reduce.31 = (bf16[1024]{0:T(1024)(128)(2,1)S(1)}, bf16[256]{0:T(256)(128)(2,1)}, bf16[1024]{0:T(1024)(128)(2,1)S(1)}) all-reduce(bf16[1024]{0:T(1024)(128)(2,1)S(1)} %dynamic-update-slice, bf16[256]{0:T(256)(128)(2,1)S(1)} %dynamic-update-slice.1, ...), channel_id=1, replica_groups=mesh['seq'=2,'shard'=16] {'shard'}, use_global_device_ids=true, to_apply=%add.23 | all-reduce | flops 2304 | bytes 9216
  53.4 17.6 all-gather
  86.0 10.8 all-gather.12.cloned.1.call-done
  104.5 44.0 %all-gather.14.cloned.1.call-done = bf16[1024,2048]{1,0:T(8,128)(2,1)} async-done(((bf16[64,2048]{1,0:T(8,128)(2,1)}), bf16[1024,2048]{1,0:T(8,128)(2,1)}) %all-gather.14.cloned.1.call-update) | async-done | bytes 4194320 | tf_op jit(solution)/shard_map/all_gather | solution.py:168
  165.0 21.2 %all-to-all-done.3 = bf16[512,8,256]{2,0,1:T(8,128)(2,1)} async-done(((bf16[512,8,256]{2,0,1:T(8,128)(2,1)}), bf16[512,8,256]{2,0,1:T(8,128)(2,1)}, u32[]{:S(2)}, u32[]{:S(2)}) %all-to-all-start.3) | async-done | bytes 2097184 | tf_op jit(solution)/shard_map/all_to_all | solution.py:202
  194.0 8.2 slice.114
  202.2 8.1 slice.115
  210.3 8.1 slice.116
  218.4 14.6 fusion.55
  255.3 316.0 %custom-call.10 = f32[4,16,1,64,64]{3,4,2,1,0:T(8,128)} custom-call(f32[4,16,1,64,64]{4,3,2,1,0:T(8,128)} %fusion.77), custom_call_target="InvertDiagBlocksLowerTriangular" | custom-call | tf_op jit(solution)/shard_map/jvp(vmap(jit(_solve_triangular)))/vmap()/triangular_solve | solution.py:100
  577.1 6.9 fusion.36
  599.4 115.8 %while.42 = (s32[]{:T(128)}, f32[4,128,256]{2,1,0:T(8,128)S(1)}, bf16[16,4,64,256]{3,2,0,1:T(8,128)(2,1)}, f32[16,4,128,256]{3,2,1,0:T(8,128)}, f32[16,4]{1,0:T(...) while((s32[]{:T(128)}, f32[4,128,256]{2,1,0:T(8,128)S(1)}, ...), condition=%wide.region_6.7_spmd.clone, body=%wide.region_5.6_spmd.clone.sunk | while | flops 353239040 | bytes 5508790 | solution.py:120
  724.8 6.6 copy.503
  731.4 18.2 all-to-all-done.4
  761.2 7.9 multiply_convert_fusion.2
  776.0 8.0 fusion.177
  784.0 7.5 fusion.178
  791.6 11.2 multiply_convert_fusion
  802.8 7.5 fusion.179
  841.3 17.0 all-to-all-done.5
  872.7 302.1 %while.43 = (s32[]{:T(128)}, f32[4,128,256]{2,1,0:T(8,128)}, f32[16,4,64,256]{3,2,1,0:T(8,128)}, f32[16,4,64,128]{3,2,1,0:T(8,128)}, f32[16,4,64,64]{3,2,0,1:T(8...) while((s32[]{:T(128)}, f32[4,128,256]{2,1,0:T(8,128)}, ...), condition=%wide.region_13.14_spmd.clone, body=%wide.region_11.13_spmd.clone.sunk | while | flops 806354944 | bytes 15272363 | solution.py:120
  1174.8 8.4 fusion.42
  1183.3 13.4 fusion.40
  1202.7 6.4 fusion.79
  1209.1 6.2 fusion.102
  1232.1 8.1 fusion.94
  1240.2 13.1 multiply_reduce_fusion.12
  1255.2 7.0 copy.515
  1262.3 15.3 add_add_fusion.3
  1277.6 19.4 multiply_reduce_fusion.4
  1318.6 12.0 add_convert_fusion
  1341.7 8.6 all-to-all-done.6
  1356.0 13.2 all_to_all.114
  1389.8 23.9 %all_to_all.115 = bf16[1024,4,256]{2,1,0:T(4,128)(2,1)S(1)} all-to-all(bf16[1024,4,256]{2,1,0:T(4,128)(2,1)S(1)} %slice_bitcast_fusion.1), channel_id=1, replica_groups=mesh['seq'=2,'shard'=16] {'seq'}, dimensions={0} | all-to-all | bytes 4194304 | tf_op jit(solution)/shard_map/all_to_all | solution.py:291
  1416.4 6.3 convolution_convert_fusion.5
  1424.0 6.8 convolution_convert_fusion.1
  1430.9 6.9 convolution_convert_fusion.2
  1439.0 6.9 convolution_convert_fusion
  1453.9 6.9 fusion.108
  1460.8 58.6 %all-reduce.29 = (f32[4,4,512]{2,1,0:T(4,128)}, f32[4,2]{0,1:T(2,128)}) all-reduce(f32[4,4,512]{2,1,0:T(4,128)S(1)} %pad_add_fusion.1, f32[4,2]{0,1:T(2,128)S(1)} %pad_add_fusion.2), channel_id=1, replica_groups=mesh['seq'=2,'shard'=16] {'shard'}, use_global_device_ids=true, to_apply=%region_43.44 | all-reduce | flops 8200 | bytes 65600 | tf_op jit(solution)/shard_map/psum | solution.py:369
  1527.1 75.1 %reduce-scatter.20.cloned.1.call-done = bf16[128,1024]{1,0:T(8,128)(2,1)} async-done(((bf16[2048,1024]{1,0:T(8,128)(2,1)}), bf16[128,1024]{1,0:T(8,128)(2,1)}) %reduce-scatter.20.cloned.1.call-update) | async-done | bytes 262160 | tf_op jit(solution)/shard_map/reduce_scatter | solution.py:339
  1602.2 75.9 %reduce-scatter.18.cloned.1.call-done = bf16[64,2048]{1,0:T(8,128)(2,1)} async-done(((bf16[1024,2048]{1,0:T(8,128)(2,1)}), bf16[64,2048]{1,0:T(8,128)(2,1)}) %reduce-scatter.18.cloned.1.call-update) | async-done | bytes 262160 | tf_op jit(solution)/shard_map/reduce_scatter | solution.py:330
  1678.2 75.0 %reduce-scatter.16.cloned.1.call-done = bf16[64,2048]{1,0:T(8,128)(2,1)} async-done(((bf16[1024,2048]{1,0:T(8,128)(2,1)}), bf16[64,2048]{1,0:T(8,128)(2,1)}) %reduce-scatter.16.cloned.1.call-update) | async-done | bytes 262160 | tf_op jit(solution)/shard_map/reduce_scatter | solution.py:327
  1753.2 84.9 %reduce-scatter.24.cloned.1.call-done = bf16[64,2816]{1,0:T(8,128)(2,1)} async-done(((bf16[1024,2816]{1,0:T(8,128)(2,1)}), bf16[64,2816]{1,0:T(8,128)(2,1)}) %reduce-scatter.24.cloned.1.call-update) | async-done | bytes 360464 | tf_op jit(solution)/shard_map/reduce_scatter | solution.py:348
  1838.1 85.0 %reduce-scatter.22.cloned.1.call-done = bf16[64,2816]{1,0:T(8,128)(2,1)} async-done(((bf16[1024,2816]{1,0:T(8,128)(2,1)}), bf16[64,2816]{1,0:T(8,128)(2,1)}) %reduce-scatter.22.cloned.1.call-update) | async-done | bytes 360464 | tf_op jit(solution)/shard_map/reduce_scatter | solution.py:345
  1923.2 85.0 %reduce-scatter.26.cloned.1.call-done = bf16[176,1024]{1,0:T(8,128)(2,1)} async-done(((bf16[2816,1024]{1,0:T(8,128)(2,1)}), bf16[176,1024]{1,0:T(8,128)(2,1)}) %reduce-scatter.26.cloned.1.call-update) | async-done | bytes 360464 | tf_op jit(solution)/shard_map/reduce_scatter | solution.py:351
  2016.5 31.6 %all-reduce.30 = (bf16[1024]{0:T(1024)(128)(2,1)S(1)}, bf16[256]{0:T(256)(128)(2,1)S(1)}, bf16[1024]{0:T(1024)(128)(2,1)S(1)}) all-reduce(bf16[1024]{0:T(1024)(128)(2,1)S(1)} %get-tuple-element.742, bf16[256]{0:T(256)(128)(2,1)S(1)} %copy-done.126, ...), channel_id=2, replica_groups=mesh['seq'=2,'shard'=16] {'shard'}, use_global_device_ids=true, to_apply=%region_27.28.clone | all-reduce | flops 2304 | bytes 9216
  2059.0 16.2 all-reduce.36.cloned.1.call-done
  (1026 shorter events, 718.1 us)
Async XLA Ops:
  7.2 63.9 %copy-start.31 = (bf16[1,512,1024]{2,1,0:T(8,128)(2,1)S(1)}, bf16[1,512,1024]{2,1,0:T(8,128)(2,1)}, u32[]{:S(2)}) copy-start(bf16[1,512,1024]{2,1,0:T(8,128)(2,1)} %param.21) | copy-start | bytes 3145732
  7.2 71.1 %all-gather.10.cloned.1.call-start = ((), (), s32[]{:S(2)}) async-start(), calls=%async_computation.19 | async-start | bytes 2228224 | tf_op jit(solution)/shard_map/all_gather | solution.py:166
  7.9 88.9 %all-gather.12.cloned.1.call-start = ((), (), s32[]{:S(2)}) async-start(), calls=%async_computation.20 | async-start | bytes 2228224 | tf_op jit(solution)/shard_map/all_gather | solution.py:167
  8.7 139.9 %all-gather.14.cloned.1.call-start = ((), (), s32[]{:S(2)}) async-start(), calls=%async_computation.21 | async-start | bytes 4456448 | tf_op jit(solution)/shard_map/all_gather | solution.py:168
  9.4 715.4 %all-gather.16.cloned.1.call-start = ((), (), s32[]{:S(2)}) async-start(), calls=%async_computation.22 | async-start | bytes 4456448 | tf_op jit(solution)/shard_map/all_gather | solution.py:169
  10.0 759.1 %all-gather.18.cloned.1.call-start = ((), (), s32[]{:S(2)}) async-start(), calls=%async_computation.23 | async-start | bytes 4456448 | tf_op jit(solution)/shard_map/all_gather | solution.py:172
  10.6 765.4 %all-gather.20.cloned.1.call-start = ((), (), s32[]{:S(2)}) async-start(), calls=%async_computation.24 | async-start | bytes 6127616 | tf_op jit(solution)/shard_map/all_gather | solution.py:176
  11.2 65.4 %copy-start.130 = (s32[1,4]{1,0:T(1,128)S(1)}, s32[1,4]{1,0:T(1,128)}, u32[]{:S(2)}) copy-start(s32[1,4]{1,0:T(1,128)} %param.22) | copy-start | bytes 52
  11.2 65.9 %copy-start.111 = (f32[4,4,512]{2,1,0:T(4,128)S(1)}, f32[4,4,512]{2,1,0:T(4,128)}, u32[]{:S(2)}) copy-start(f32[4,4,512]{2,1,0:T(4,128)} %param.29) | copy-start | bytes 98308
  11.2 772.9 %all-gather.22.cloned.1.call-start = ((), (), s32[]{:S(2)}) async-start(), calls=%async_computation.25 | async-start | bytes 6127616 | tf_op jit(solution)/shard_map/all_gather | solution.py:177
  53.4 707.8 %copy-start.104 = (f32[1024]{0:T(1024)}, f32[1024]{0:T(1024)S(1)}, u32[]{:S(2)}) copy-start(f32[1024]{0:T(1024)S(1)} %convert_element_type.312) | copy-start | bytes 12292
  71.4 689.8 %copy-start.114 = (f32[512]{0:T(512)}, f32[512]{0:T(512)S(1)}, u32[]{:S(2)}) copy-start(f32[512]{0:T(512)S(1)} %fusion.153) | copy-start | bytes 6148
  72.5 9.8 all-to-all-start
  75.8 715.8 %all-gather.24.cloned.1.call-start = ((), (), s32[]{:S(2)}) async-start(), calls=%async_computation.26 | async-start | bytes 6127616 | tf_op jit(solution)/shard_map/all_gather | solution.py:178
  77.1 141.3 %copy-start.94 = (f32[4,512]{1,0:T(4,128)}, f32[4,512]{1,0:T(4,128)S(1)}, u32[]{:S(2)}) copy-start(f32[4,512]{1,0:T(4,128)S(1)} %get-tuple-element.856) | copy-start | bytes 24580
  77.1 141.3 %copy-start.96 = (f32[4,512]{1,0:T(4,128)}, f32[4,512]{1,0:T(4,128)S(1)}, u32[]{:S(2)}) copy-start(f32[4,512]{1,0:T(4,128)S(1)} %get-tuple-element.857) | copy-start | bytes 24580
  77.1 141.3 %copy-start.98 = (f32[4,512]{1,0:T(4,128)}, f32[4,512]{1,0:T(4,128)S(1)}, u32[]{:S(2)}) copy-start(f32[4,512]{1,0:T(4,128)S(1)} %get-tuple-element.855) | copy-start | bytes 24580
  77.1 141.3 %copy-start.100 = (f32[4,512]{1,0:T(4,128)}, f32[4,512]{1,0:T(4,128)S(1)}, u32[]{:S(2)}) copy-start(f32[4,512]{1,0:T(4,128)S(1)} %get-tuple-element.858) | copy-start | bytes 24580
  77.2 174.5 %copy-start.86 = (pred[64,64]{1,0:T(8,128)(4,1)}, pred[64,64]{1,0:T(8,128)(4,1)S(1)}, u32[]{:S(2)}) copy-start(pred[64,64]{1,0:T(8,128)(4,1)S(1)} %get-tuple-element.885) | copy-start | bytes 12292
  77.6 174.1 %copy-start.56 = (pred[16,64,64]{2,1,0:T(8,128)(4,1)}, pred[16,64,64]{2,1,0:T(8,128)(4,1)S(1)}, u32[]{:S(2)}) copy-start(pred[16,64,64]{2,1,0:T(8,128)(4,1)S(1)} %get-tuple-element.862) | copy-start | bytes 196612
  77.6 515.9 %copy-start.49 = (pred[16,64,64]{2,1,0:T(8,128)(4,1)}, pred[16,64,64]{2,1,0:T(8,128)(4,1)S(1)}, u32[]{:S(2)}) copy-start(pred[16,64,64]{2,1,0:T(8,128)(4,1)S(1)} %get-tuple-element.861) | copy-start | bytes 196612
  82.4 18.6 all-to-all-start.1
  86.0 76.5 %copy-start.92 = (f32[16,64]{1,0:T(8,128)}, f32[16,64]{1,0:T(8,128)S(1)}, u32[]{:S(2)}) copy-start(f32[16,64]{1,0:T(8,128)S(1)} %get-tuple-element.864) | copy-start | bytes 12292
  86.0 76.5 %copy-start.106 = (pred[16,64]{1,0:T(8,128)(4,1)}, pred[16,64]{1,0:T(8,128)(4,1)S(1)}, u32[]{:S(2)}) copy-start(pred[16,64]{1,0:T(8,128)(4,1)S(1)} %get-tuple-element.863) | copy-start | bytes 3076
  100.9 53.7 %all-to-all-start.2 = ((bf16[512,8,128]{2,0,1:T(8,128)(2,1)}), bf16[512,8,128]{2,0,1:T(8,128)(2,1)S(1)}, u32[]{:S(2)}, u32[]{:S(2)}) async-start(bf16[512,8,128]{2,0,1:T(8,128)(2,1)} %bitcast.545), calls=%async_computation.2 | async-start | bytes 2097152 | tf_op jit(solution)/shard_map/all_to_all | solution.py:199
  155.6 30.7 %all-to-all-start.3 = ((bf16[512,8,256]{2,0,1:T(8,128)(2,1)}), bf16[512,8,256]{2,0,1:T(8,128)(2,1)}, u32[]{:S(2)}, u32[]{:S(2)}) async-start(bf16[512,8,256]{2,0,1:T(8,128)(2,1)} %bitcast.422), calls=%async_computation.3 | async-start | bytes 4194304 | tf_op jit(solution)/shard_map/all_to_all | solution.py:202
  161.0 410.3 %copy-start.51 = (f32[4,16,64]{2,1,0:T(8,128)}, f32[4,16,64]{2,1,0:T(8,128)S(1)}, u32[]{:S(2)}) copy-start(f32[4,16,64]{2,1,0:T(8,128)S(1)} %div.80) | copy-start | bytes 49156
  162.4 431.1 %copy-start.29 = (f32[4,16,64]{2,1,0:T(8,128)}, f32[4,16,64]{2,1,0:T(8,128)S(1)}, u32[]{:S(2)}) copy-start(f32[4,16,64]{2,1,0:T(8,128)S(1)} %reduce_window_sum.22) | copy-start | bytes 49156
  162.7 412.0 %copy-start.70 = (f32[4,16,64]{2,1,0:T(8,128)}, f32[4,16,64]{2,1,0:T(8,128)S(1)}, u32[]{:S(2)}) copy-start(f32[4,16,64]{2,1,0:T(8,128)S(1)} %get-tuple-element.848) | copy-start | bytes 49156
  162.7 412.0 %copy-start.73 = (f32[4,16,64]{2,1,0:T(8,128)}, f32[4,16,64]{2,1,0:T(8,128)S(1)}, u32[]{:S(2)}) copy-start(f32[4,16,64]{2,1,0:T(8,128)S(1)} %get-tuple-element.847) | copy-start | bytes 49156
  162.7 412.0 %copy-start.75 = (f32[4,16,64]{2,1,0:T(8,128)}, f32[4,16,64]{2,1,0:T(8,128)S(1)}, u32[]{:S(2)}) copy-start(f32[4,16,64]{2,1,0:T(8,128)S(1)} %get-tuple-element.852) | copy-start | bytes 49156
  163.8 54.6 %copy-start.21 = (bf16[2,512,4,128]{3,2,1,0:T(4,128)(2,1)}, bf16[2,512,4,128]{3,2,1,0:T(4,128)(2,1)S(1)}, u32[]{:S(2)}) copy-start(bf16[2,512,4,128]{3,2,1,0:T(4,128)(2,1)S(1)} %copy.479) | copy-start | bytes 3145732
  719.8 29.8 %all-to-all-start.4 = ((bf16[1024,4,256]{2,1,0:T(4,128)(2,1)}), bf16[1024,4,256]{2,1,0:T(4,128)(2,1)}, u32[]{:S(2)}, u32[]{:S(2)}) async-start(bf16[1024,4,256]{2,1,0:T(4,128)(2,1)} %copy.500), calls=%async_computation.4 | async-start | bytes 4194304 | tf_op jit(solution)/shard_map/all_to_all | solution.py:227
  829.5 28.8 %all-to-all-start.5 = ((bf16[512,8,256]{0,2,1:T(8,128)(2,1)}), bf16[512,8,256]{0,2,1:T(8,128)(2,1)}, u32[]{:S(2)}, u32[]{:S(2)}) async-start(bf16[512,8,256]{0,2,1:T(8,128)(2,1)} %get-tuple-element.829), calls=%async_computation.5 | async-start | bytes 4194304 | tf_op jit(solution)/shard_map/all_to_all | solution.py:278
  1315.4 19.4 all-to-all-start.9
  1334.8 15.4 all-to-all-start.6
  1338.6 180.8 %reduce-scatter.28.cloned.1.call-start = ((), (), s32[]{:S(2)}) async-start(), calls=%async_computation.35 | async-start | bytes 278528
  1341.7 182.8 %reduce-scatter.12.cloned.1.call-start = ((), (), s32[]{:S(2)}) async-start(), calls=%async_computation.27 | async-start | bytes 2228224 | tf_op jit(solution)/shard_map/reduce_scatter | solution.py:321
  1354.8 172.3 %reduce-scatter.14.cloned.1.call-start = ((), (), s32[]{:S(2)}) async-start(), calls=%async_computation.28 | async-start | bytes 2228224 | tf_op jit(solution)/shard_map/reduce_scatter | solution.py:324
  1373.7 228.5 %reduce-scatter.20.cloned.1.call-start = ((), (), s32[]{:S(2)}) async-start(), calls=%async_computation.31 | async-start | bytes 4456448 | tf_op jit(solution)/shard_map/reduce_scatter | solution.py:339
  1381.2 296.9 %reduce-scatter.18.cloned.1.call-start = ((), (), s32[]{:S(2)}) async-start(), calls=%async_computation.30 | async-start | bytes 4456448 | tf_op jit(solution)/shard_map/reduce_scatter | solution.py:330
  1387.5 365.7 %reduce-scatter.16.cloned.1.call-start = ((), (), s32[]{:S(2)}) async-start(), calls=%async_computation.29 | async-start | bytes 4456448 | tf_op jit(solution)/shard_map/reduce_scatter | solution.py:327
  1422.8 415.4 %reduce-scatter.24.cloned.1.call-start = ((), (), s32[]{:S(2)}) async-start(), calls=%async_computation.33 | async-start | bytes 6127616 | tf_op jit(solution)/shard_map/reduce_scatter | solution.py:348
  1430.8 492.4 %reduce-scatter.22.cloned.1.call-start = ((), (), s32[]{:S(2)}) async-start(), calls=%async_computation.32 | async-start | bytes 6127616 | tf_op jit(solution)/shard_map/reduce_scatter | solution.py:345
  1437.8 570.4 %reduce-scatter.26.cloned.1.call-start = ((), (), s32[]{:S(2)}) async-start(), calls=%async_computation.34 | async-start | bytes 6127616 | tf_op jit(solution)/shard_map/reduce_scatter | solution.py:351
  1445.9 629.2 %all-reduce.36.cloned.1.call-start = ((), (), s32[]{:S(2)}) async-start(), calls=%async_computation.36 | async-start | bytes 4259840 | tf_op jit(solution)/shard_map/psum | solution.py:357
  1453.9 66.3 %copy-start.67 = (bf16[512,2,4,128]{0,3,2,1:T(8,128)(2,1)S(1)}, bf16[512,2,4,128]{0,3,2,1:T(8,128)(2,1)}, u32[]{:S(2)}) copy-start(bf16[512,2,4,128]{0,3,2,1:T(8,128)(2,1)} %copy-done.66) | copy-start | bytes 3145732
  1524.5 483.8 %copy-start.65 = (bf16[512,2,4,128]{0,3,2,1:T(8,128)(2,1)S(1)}, bf16[512,2,4,128]{0,3,2,1:T(8,128)(2,1)}, u32[]{:S(2)}) copy-start(bf16[512,2,4,128]{0,3,2,1:T(8,128)(2,1)} %copy-done.64) | copy-start | bytes 3145732
  (163 other events, 986.6 us)
Sparse Core Ops, SparseCore 0:
  10.2 44.2 all-gather.9
  56.6 40.1 all-gather.11
  99.0 49.4 all-gather.13
  150.6 49.1 all-gather.15
  201.7 49.0 all-gather.17
  252.9 57.9 all-gather.19
  313.2 59.0 all-gather.21
  374.6 58.1 all-gather.23
  1343.5 54.4 reduce-scatter.27
  1401.5 60.5 reduce-scatter.11
  1466.4 60.6 reduce-scatter.13
  1530.8 71.3 reduce-scatter.19
  1606.6 71.5 reduce-scatter.17
  1681.9 71.2 reduce-scatter.15
  1757.4 80.6 reduce-scatter.23
  1842.4 80.7 reduce-scatter.21
  1927.4 80.7 reduce-scatter.25
  2011.0 64.1 all-reduce.35
where the time goes:
time: 2110 us; the launch traced here: 2090 us
  waiting for transfers between devices  625 us (30%)
  other arithmetic  503 us (24%)
  matrix products  445 us (21%)
  local copies, waits for them, and re-layouts  277 us (13%)
  blocking collectives  186 us (9%)
  starting transfers between devices  33.2 us (2%)
    another operation x5, other arithmetic, delta_rule(): jax.scipy.linalg.solve_triangular(system, right_side, lower=True, unit_di...  318 us
    dot_general x208, matrix products, product(): jnp.dot(left_side, right_side, precision=highest, preferred_element_type=...  246 us
    squeeze x96, local copies, waits for them, and re-layouts, delta_rule(): lax.scan(jax.checkpoint(advance), start, (new_values, corrections, scores...  101 us
    reduce_scatter x1, waiting for transfers between devices, on_device(): lax.psum_scatter(ffn_gate_grad.astype(jnp.bfloat16), 'shard', scatter_dim...  85 us
    reduce_scatter x1, waiting for transfers between devices, on_device(): lax.psum_scatter(down_grad.astype(jnp.bfloat16), 'shard', scatter_dimensi...  85 us
    reduce_scatter x1, waiting for transfers between devices, on_device(): lax.psum_scatter(ffn_up_grad.astype(jnp.bfloat16), 'shard', scatter_dimen...  84.9 us
    reduce_scatter x1, waiting for transfers between devices, on_device(): lax.psum_scatter(gate_weight_grad.astype(jnp.bfloat16), 'shard', scatter_...  75.9 us
    reduce_scatter x1, waiting for transfers between devices, on_device(): lax.psum_scatter(out_grad.astype(jnp.bfloat16), 'shard', scatter_dimensio...  75.1 us
  transfers between devices with their start and end apart: 26, of which 14 were waited for; matrix products, arithmetic and copies ran while one was open for 34% of the time, Pallas kernels for 0%

commit v1 on v0

v1 whole, which is shorter than its diff:
```python
import functools

import jax
import jax.numpy as jnp
from jax import lax
from jax.experimental import pallas as pl
from jax.experimental.pallas import tpu as pltpu
from jax.sharding import PartitionSpec as P

HEADS = 8
KEY = 128
VALUE = 256
CONV = 4
GROUP = 64
HALO = 16
SUB = 4
epsilon = 1e-06
f32 = jnp.float32
bf16 = jnp.bfloat16


def dot(a, b, ca=1, cb=0):
    return lax.dot_general(a, b, (((ca,), (cb,)), ((), ())), preferred_element_type=f32)


def iota(shape, dim):
    return lax.broadcasted_iota(jnp.int32, shape, dim)


def doc_count(starts_ref, times):
    count = jnp.zeros(times.shape, jnp.int32)
    for s in range(starts_ref.shape[1]):
        count = count + jnp.where(times >= starts_ref[0, s], 1, 0)
    return count


def scalar_doc(starts_ref, time):
    count = 0
    for s in range(starts_ref.shape[1]):
        count = count + (time >= starts_ref[0, s]).astype(jnp.int32)
    return count


def per_head(cols, heads, width):
    rows = cols.shape[0]
    lane = iota((rows, heads * width), 1)
    out = jnp.broadcast_to(cols[:, heads - 1 : heads], (rows, heads * width))
    for h in range(heads - 2, -1, -1):
        out = jnp.where(lane < (h + 1) * width, cols[:, h : h + 1], out)
    return out


def head_sums(panel, heads, width):
    lane = iota(panel.shape, 1)
    sums = []
    for h in range(heads):
        inside = (lane >= h * width) & (lane < (h + 1) * width)
        sums.append(jnp.sum(jnp.where(inside, panel, 0.0), axis=1, keepdims=True))
    return columns(sums)


def columns(parts):
    rows = parts[0].shape[0]
    lane = iota((rows, len(parts)), 1)
    out = jnp.broadcast_to(parts[-1], (rows, len(parts)))
    for h in range(len(parts) - 2, -1, -1):
        out = jnp.where(lane == h, parts[h], out)
    return out


def block_diagonal(panel, heads):
    if heads == 1:
        return panel
    lane = iota(panel.shape, 1)
    zero = jnp.zeros_like(panel)
    parts = []
    for h in range(heads):
        inside = (lane >= h * GROUP) & (lane < (h + 1) * GROUP)
        parts.append(jnp.where(inside, panel, zero))
    return jnp.concatenate(parts, axis=0)


def diagonal_panel(full, heads):
    if heads == 1:
        return full
    lane = iota((GROUP, heads * GROUP), 1)
    out = full[(heads - 1) * GROUP :]
    for h in range(heads - 2, -1, -1):
        out = jnp.where(lane < (h + 1) * GROUP, full[h * GROUP : (h + 1) * GROUP], out)
    return out


def key_diagonal(keys):
    heads = len(keys)
    if heads == 1:
        return keys[0]
    zero = jnp.zeros_like(keys[0])
    rows = []
    for h in range(heads):
        rows.append(jnp.concatenate([keys[h] if o == h else zero for o in range(heads)], axis=1))
    return jnp.concatenate(rows, axis=0)


def scan_rows(values, reverse=False):
    rows = values.shape[0]
    index = iota(values.shape, 0)
    step = 1
    while step < rows:
        if reverse:
            moved = pltpu.roll(values, rows - step, 0)
            values = values + jnp.where(index < rows - step, moved, 0.0)
        else:
            moved = pltpu.roll(values, step, 0)
            values = values + jnp.where(index >= step, moved, 0.0)
        step *= 2
    return values


def sigmoid(v):
    return 1.0 / (1.0 + jnp.exp(-v))


def softplus(v):
    return jnp.maximum(v, 0.0) + jnp.log(1.0 + jnp.exp(-jnp.abs(v)))


class Block:
    def __init__(self, heads, base, raw_ref, filters_ref, decay_ref, starts_ref, backward=False):
        self.heads = heads
        width = heads * (2 * KEY + VALUE)
        times = base + iota((GROUP, 1), 0)
        docs = doc_count(starts_ref, times)
        self.masks = [
            (docs == doc_count(starts_ref, times - o)).astype(f32) for o in range(1, CONV)
        ]
        self.base = base
        self.raw_ref = raw_ref
        self.filters_ref = filters_ref
        self.query, self.keys, self.query_pre, self.key_pre = [], [], [], []
        self.query_conv, self.key_conv, self.query_scale, self.key_scale = [], [], [], []
        for h in range(heads):
            pre = self.convolve(h * KEY, KEY)
            conv = pre * sigmoid(pre)
            scale = lax.rsqrt(jnp.sum(conv * conv, axis=1, keepdims=True) + epsilon)
            self.query_pre.append(pre)
            self.query_conv.append(conv)
            self.query_scale.append(scale)
            self.query.append(conv * scale * KEY ** (-0.5))
        for h in range(heads):
            pre = self.convolve((heads + h) * KEY, KEY)
            conv = pre * sigmoid(pre)
            scale = lax.rsqrt(jnp.sum(conv * conv, axis=1, keepdims=True) + epsilon)
            self.key_pre.append(pre)
            self.key_conv.append(conv)
            self.key_scale.append(scale)
            self.keys.append(conv * scale)
        logits = raw_ref[pl.ds(base, GROUP), width : width + 2 * KEY // 2].astype(f32)
        self.strength = sigmoid(logits[:, :heads])
        self.decay_logit = logits[:, heads : 2 * heads] + decay_ref[1:2, :heads]
        self.decay_rate = -jnp.exp(decay_ref[0:1, :heads])
        self.log_decay = self.decay_rate * softplus(self.decay_logit)
        sums = scan_rows(self.log_decay)
        self.sums = sums
        last = sums[GROUP - 1 : GROUP]
        before = scalar_doc(starts_ref, base - 1)
        final = scalar_doc(starts_ref, base + GROUP - 1)
        self.entering = jnp.where(docs == before, jnp.exp(sums), 0.0)
        same_last = docs == final
        self.leaving = jnp.where(same_last, jnp.exp(jnp.where(same_last, last - sums, 0.0)), 0.0)
        self.retain = self.entering[GROUP - 1 : GROUP]
        shape = (GROUP, heads * GROUP)
        row = iota(shape, 0)
        place = jnp.bitwise_and(iota(shape, 1), GROUP - 1)
        self.row, self.place = row, place
        across = jnp.bitwise_and(iota((1, heads * GROUP), 1), GROUP - 1)
        docs_across = doc_count(starts_ref, base + across)
        same = docs == docs_across
        self.inclusive = same & (row >= place)
        self.strict = same & (row > place)
        sums_down = per_head(sums, heads, GROUP)
        sums_across = jnp.sum(jnp.where(row == place, sums_down, 0.0), axis=0, keepdims=True)
        gap = jnp.where(self.inclusive, sums_down - sums_across, 0.0)
        self.fade = jnp.where(self.inclusive, jnp.exp(gap), 0.0)
        self.strength_down = per_head(self.strength, heads, GROUP)
        low_keys = [k.astype(bf16) for k in self.keys]
        low_query = [q.astype(bf16) for q in self.query]
        self.low_keys, self.low_query = low_keys, low_query
        self.key_diag = key_diagonal(low_keys)
        left = jnp.concatenate(
            [jnp.concatenate(low_keys, axis=1), jnp.concatenate(low_query, axis=1)], axis=0
        )
        self.query_key_rows = left
        grams = dot(left, self.key_diag, 1, 1)
        self.key_gram = grams[:GROUP]
        self.score_gram = grams[GROUP:]
        self.system = jnp.where(self.strict, self.strength_down * self.key_gram * self.fade, 0.0)
        self.scores = self.score_gram * self.fade

    def taps(self, start, width):
        current = self.raw_ref[pl.ds(self.base, GROUP), start : start + width].astype(f32)
        earlier = pl.multiple_of(jnp.maximum(self.base - HALO, 0), HALO)
        halo = self.raw_ref[pl.ds(earlier, HALO), start : start + width].astype(f32)
        extended = jnp.concatenate([halo, current], axis=0)
        return [current] + [
            pltpu.roll(extended, o, 0)[HALO:] * self.masks[o - 1] for o in range(1, CONV)
        ]

    def convolve(self, start, width):
        taps = self.taps(start, width)
        filters = self.filters_ref[:, start : start + width]
        total = taps[0] * filters[CONV - 1 : CONV]
        for o in range(1, CONV):
            total = total + taps[o] * filters[CONV - 1 - o : CONV - o]
        return total


def inverse(system, heads, row, place):
    eye = (row == place).astype(f32)

    def part(size):
        apart = jnp.bitwise_xor(row, place)
        return jnp.where((apart >= size) & (apart < 2 * size), system, 0.0)

    result = eye - part(1)
    size = 2
    while size < GROUP:
        low = result.astype(bf16)
        inner = dot(part(size).astype(bf16), block_diagonal(low, heads))
        result = result - dot(low, block_diagonal(inner.astype(bf16), heads))
        size *= 2
    return result


def forward_kernel(
    heads, starts_ref, raw_ref, filters_ref, decay_ref,
    mixed_ref, inverse_ref, delta_ref, rest_ref, memory_ref, state,
):
    step = pl.program_id(0)

    @pl.when(step == 0)
    def _():
        state[...] = jnp.zeros_like(state)

    blocks = []
    for s in range(SUB):
        base = pl.multiple_of((step * SUB + s) * GROUP, GROUP)
        block = Block(heads, base, raw_ref, filters_ref, decay_ref, starts_ref)
        block.values = []
        for h in range(heads):
            pre = block.convolve(2 * heads * KEY + h * VALUE, VALUE)
            block.values.append(pre * sigmoid(pre))
        block.solve = inverse(block.system, heads, block.row, block.place).astype(bf16)
        inverse_ref[s * GROUP : (s + 1) * GROUP] = block.solve
        blocks.append(block)
    for s, block in enumerate(blocks):
        from_state, rest, right = [], [], []
        for h in range(heads):
            entering = block.entering[:, h : h + 1]
            memory = state[h * KEY : (h + 1) * KEY].astype(bf16)
            memory_ref[(s * heads + h) * KEY : (s * heads + h + 1) * KEY] = memory
            both = jnp.concatenate([entering * block.keys[h], entering * block.query[h]], axis=0)
            read = dot(both.astype(bf16), memory)
            from_state.append(read[GROUP:])
            missing = block.values[h] - read[:GROUP]
            rest.append(missing.astype(bf16))
            right.append((block.strength[:, h : h + 1] * missing).astype(bf16))
        rest_ref[s * heads * GROUP : (s + 1) * heads * GROUP] = jnp.concatenate(rest, axis=0)
        delta = dot(block_diagonal(block.solve, heads), jnp.concatenate(right, axis=0)).astype(bf16)
        delta_ref[s * heads * GROUP : (s + 1) * heads * GROUP] = delta
        outputs = dot(block_diagonal(block.scores.astype(bf16), heads), delta)
        for h in range(heads):
            rows = slice(h * GROUP, (h + 1) * GROUP)
            out = from_state[h] + outputs[rows]
            mixed_ref[s * GROUP : (s + 1) * GROUP, h * VALUE : (h + 1) * VALUE] = out.astype(bf16)
            leaving = (block.leaving[:, h : h + 1] * block.keys[h]).astype(bf16)
            keep = block.retain[:, h : h + 1]
            own = slice(h * KEY, (h + 1) * KEY)
            state[own] = keep * state[own] + dot(leaving, delta[rows], 0, 0)


def silu_slope(pre):
    gate = sigmoid(pre)
    return gate * (1.0 + pre * (1.0 - gate))


def backward_kernel(
    heads, starts_ref, raw_ref, filters_ref, decay_ref,
    mixed_grad_ref, inverse_ref, delta_ref, rest_ref, memory_ref,
    raw_grad_ref, filters_grad_ref, decay_grad_ref, state, halo,
):
    step = pl.program_id(0)
    steps = pl.num_programs(0)
    width = heads * (2 * KEY + VALUE)

    @pl.when(step == 0)
    def _():
        state[...] = jnp.zeros_like(state)
        halo[...] = jnp.zeros_like(halo)
        filters_grad_ref[...] = jnp.zeros_like(filters_grad_ref)
        decay_grad_ref[...] = jnp.zeros_like(decay_grad_ref)

    for s in range(SUB - 1, -1, -1):
        base = pl.multiple_of(((steps - 1 - step) * SUB + s) * GROUP, GROUP)
        block = Block(heads, base, raw_ref, filters_ref, decay_ref, starts_ref)
        here = slice(s * GROUP, (s + 1) * GROUP)
        stacked = slice(s * heads * GROUP, (s + 1) * heads * GROUP)
        solve = inverse_ref[here]
        delta = delta_ref[stacked]
        rest = rest_ref[stacked]
        out_grad = jnp.concatenate(
            [mixed_grad_ref[here, h * VALUE : (h + 1) * VALUE] for h in range(heads)], axis=0
        )
        later = [state[h * KEY : (h + 1) * KEY] for h in range(heads)]
        later_low = [m.astype(bf16) for m in later]
        leaving = [
            (block.leaving[:, h : h + 1] * block.keys[h]).astype(bf16) for h in range(heads)
        ]
        pulled = jnp.concatenate([dot(leaving[h], later_low[h]) for h in range(heads)], axis=0)
        delta_grad = pulled + dot(block_diagonal(block.scores.astype(bf16), heads), out_grad, 0, 0)
        right_grad = dot(block_diagonal(solve, heads), delta_grad.astype(bf16), 0, 0)
        rest_grad, strength_grad = [], []
        for h in range(heads):
            rows = slice(h * GROUP, (h + 1) * GROUP)
            rest_grad.append(block.strength[:, h : h + 1] * right_grad[rows])
            strength_grad.append(
                jnp.sum(right_grad[rows] * rest[rows].astype(f32), axis=1, keepdims=True)
            )
        rest_low = [r.astype(bf16) for r in rest_grad]
        entering_query_grad, entering_key_grad, leaving_key_grad, retain_grad = [], [], [], []
        for h in range(heads):
            rows = slice(h * GROUP, (h + 1) * GROUP)
            entering = block.entering[:, h : h + 1]
            memory = memory_ref[(s * heads + h) * KEY : (s * heads + h + 1) * KEY]
            pair = jnp.concatenate([out_grad[rows], rest_low[h]], axis=0)
            back = dot(pair, memory, 1, 1)
            entering_query_grad.append(back[:GROUP])
            entering_key_grad.append(-back[GROUP:])
            leaving_key_grad.append(dot(delta[rows], later_low[h], 1, 1))
            product = later[h] * memory.astype(f32)
            retain_grad.append(
                jnp.sum(jnp.sum(product, axis=0, keepdims=True), axis=1, keepdims=True)
            )
            left = jnp.concatenate(
                [entering * block.query[h], -entering * block.keys[h]], axis=0
            ).astype(bf16)
            state[h * KEY : (h + 1) * KEY] = (
                block.retain[:, h : h + 1] * later[h] + dot(left, pair, 0, 0)
            )
        right_low = right_grad.astype(bf16)
        score_part = diagonal_panel(dot(out_grad, delta, 1, 1), heads)
        system_part = diagonal_panel(dot(right_low, delta, 1, 1), heads)
        scores_grad = jnp.where(block.inclusive, score_part, 0.0)
        system_grad = jnp.where(block.strict, -system_part, 0.0)
        score_gram_grad = scores_grad * block.fade
        faded = system_grad * block.fade
        key_gram_grad = block.strength_down * faded
        gap_grad = score_gram_grad * block.score_gram + key_gram_grad * block.key_gram
        strength_panel = head_sums(faded * block.key_gram, heads, GROUP)
        down = jnp.sum(gap_grad, axis=0, keepdims=True)
        gap_rows = head_sums(
            gap_grad - jnp.where(block.row == block.place, down, 0.0), heads, GROUP
        )
        both_low = jnp.concatenate([key_gram_grad, score_gram_grad], axis=0).astype(bf16)
        straight = dot(both_low, block.key_diag)
        turned = dot(both_low, block.query_key_rows, 0, 0)
        entering_grad, leaving_grad = [], []
        for h in range(heads):
            lanes = slice(h * KEY, (h + 1) * KEY)
            entering = block.entering[:, h : h + 1]
            fading = block.leaving[:, h : h + 1]
            query_grad = entering * entering_query_grad[h] + straight[GROUP:, lanes]
            key_grad = (
                turned[h * GROUP : (h + 1) * GROUP, lanes]
                + straight[:GROUP, lanes]
                + fading * leaving_key_grad[h]
                + entering * entering_key_grad[h]
            )
            entering_grad.append(
                jnp.sum(
                    entering_query_grad[h] * block.query[h] + entering_key_grad[h] * block.keys[h],
                    axis=1,
                    keepdims=True,
                )
            )
            leaving_grad.append(
                jnp.sum(leaving_key_grad[h] * block.keys[h], axis=1, keepdims=True)
            )
            for start, grad, conv, scale, pre, factor in (
                (h * KEY, query_grad, block.query_conv[h], block.query_scale[h],
                 block.query_pre[h], KEY ** (-0.5)),
                ((heads + h) * KEY, key_grad, block.key_conv[h], block.key_scale[h],
                 block.key_pre[h], 1.0),
            ):
                along = jnp.sum(grad * conv, axis=1, keepdims=True)
                conv_grad = (factor * scale) * (grad - conv * (scale * scale * along))
                convolve_back(
                    block, s, start, KEY, conv_grad * silu_slope(pre), starts_ref,
                    raw_grad_ref, filters_grad_ref, halo,
                )
            start = 2 * heads * KEY + h * VALUE
            pre = block.convolve(start, VALUE)
            convolve_back(
                block, s, start, VALUE, rest_grad[h] * silu_slope(pre), starts_ref,
                raw_grad_ref, filters_grad_ref, halo,
            )
        entering_grad = columns(entering_grad) * block.entering
        leaving_grad = columns(leaving_grad) * block.leaving
        strength_grad = columns(strength_grad) + strength_panel
        retain_grad = columns(retain_grad) * block.retain
        at_last = jnp.sum(leaving_grad, axis=0, keepdims=True) + retain_grad
        index = iota((GROUP, heads), 0)
        sums_grad = (
            entering_grad - leaving_grad + gap_rows + jnp.where(index == GROUP - 1, at_last, 0.0)
        )
        log_decay_grad = scan_rows(sums_grad, reverse=True)
        logit_grad = log_decay_grad * block.decay_rate * sigmoid(block.decay_logit)
        beta_grad = strength_grad * block.strength * (1.0 - block.strength)
        lane = iota((GROUP, KEY), 1)
        packed = jnp.zeros((GROUP, KEY), f32)
        for h in range(heads):
            packed = jnp.where(lane == h, beta_grad[:, h : h + 1], packed)
            packed = jnp.where(lane == heads + h, logit_grad[:, h : h + 1], packed)
        raw_grad_ref[here, width : width + KEY] = packed.astype(bf16)
        scale_sum = jnp.sum(log_decay_grad * block.log_decay, axis=0, keepdims=True)
        bias_sum = jnp.sum(logit_grad, axis=0, keepdims=True)
        decay_grad_ref[0:1] = decay_grad_ref[0:1] + scale_sum
        decay_grad_ref[1:2] = decay_grad_ref[1:2] + bias_sum


def convolve_back(
    block, s, start, width, pre_grad, starts_ref, raw_grad_ref, filters_grad_ref, halo
):
    lanes = slice(start, start + width)
    taps = block.taps(start, width)
    for o in range(CONV):
        j = CONV - 1 - o
        product = (pre_grad * taps[o]).reshape(GROUP // 8, 8, width)
        filters_grad_ref[j * 8 : (j + 1) * 8, lanes] = filters_grad_ref[
            j * 8 : (j + 1) * 8, lanes
        ] + jnp.sum(product, axis=0)
    filters = block.filters_ref[:, lanes]
    extended = jnp.concatenate([pre_grad, halo[:, lanes]], axis=0)
    rows = GROUP + 8
    times = block.base + iota((rows, 1), 0)
    docs = doc_count(starts_ref, times)
    total = pre_grad * filters[CONV - 1 : CONV]
    for o in range(1, CONV):
        mask = (docs == doc_count(starts_ref, times - o)).astype(f32)
        moved = pltpu.roll(extended * mask, rows - o, 0)[:GROUP]
        total = total + moved * filters[CONV - 1 - o : CONV - o]
    raw_grad_ref[s * GROUP : (s + 1) * GROUP, lanes] = total.astype(bf16)
    halo[:, lanes] = pre_grad[:8]


SPACE = 56 * 2**20


def mixer_forward(raw, filters, decays, starts, heads):
    length, wide = raw.shape
    steps = length // (SUB * GROUP)
    rows = SUB * GROUP
    blocks = length // GROUP
    whole = lambda a: pl.BlockSpec(a.shape, lambda i: (0, 0))
    part = lambda r, c: pl.BlockSpec((r, c), lambda i: (i, 0))
    return pl.pallas_call(
        functools.partial(forward_kernel, heads),
        grid=(steps,),
        in_specs=[
            pl.BlockSpec(memory_space=pltpu.SMEM), whole(raw), whole(filters), whole(decays),
        ],
        out_specs=[
            part(rows, heads * VALUE), part(rows, heads * GROUP), part(rows * heads, VALUE),
            part(rows * heads, VALUE), part(SUB * heads * KEY, VALUE),
        ],
        out_shape=[
            jax.ShapeDtypeStruct((length, heads * VALUE), bf16),
            jax.ShapeDtypeStruct((length, heads * GROUP), bf16),
            jax.ShapeDtypeStruct((length * heads, VALUE), bf16),
            jax.ShapeDtypeStruct((length * heads, VALUE), bf16),
            jax.ShapeDtypeStruct((blocks * heads * KEY, VALUE), bf16),
        ],
        scratch_shapes=[pltpu.VMEM((heads * KEY, VALUE), f32)],
        compiler_params=pltpu.CompilerParams(vmem_limit_bytes=SPACE),
        name="mixer_forward",
    )(starts, raw, filters, decays)


def mixer_backward(raw, filters, decays, starts, mixed_grad, kept, heads):
    length, wide = raw.shape
    steps = length // (SUB * GROUP)
    rows = SUB * GROUP
    whole = lambda a: pl.BlockSpec(a.shape, lambda i: (0, 0))
    part = lambda r, c: pl.BlockSpec((r, c), lambda i: (steps - 1 - i, 0))
    return pl.pallas_call(
        functools.partial(backward_kernel, heads),
        grid=(steps,),
        in_specs=[
            pl.BlockSpec(memory_space=pltpu.SMEM), whole(raw), whole(filters), whole(decays),
            part(rows, heads * VALUE), part(rows, heads * GROUP), part(rows * heads, VALUE),
            part(rows * heads, VALUE), part(SUB * heads * KEY, VALUE),
        ],
        out_specs=[
            part(rows, wide),
            pl.BlockSpec((8 * CONV, filters.shape[1]), lambda i: (0, 0)),
            pl.BlockSpec((2, heads), lambda i: (0, 0)),
        ],
        out_shape=[
            jax.ShapeDtypeStruct((length, wide), bf16),
            jax.ShapeDtypeStruct((8 * CONV, filters.shape[1]), f32),
            jax.ShapeDtypeStruct((2, heads), f32),
        ],
        scratch_shapes=[
            pltpu.VMEM((heads * KEY, VALUE), f32),
            pltpu.VMEM((8, filters.shape[1]), f32),
        ],
        compiler_params=pltpu.CompilerParams(vmem_limit_bytes=SPACE),
        name="mixer_backward",
    )(starts, raw, filters, decays, mixed_grad, *kept)


def forward_dot(left_side, right_side):
    return jnp.dot(left_side, right_side, preferred_element_type=f32)


def times_transposed(left_side, right_side):
    return dot(left_side, right_side, 1, 1)


def transposed_times(left_side, right_side):
    return dot(left_side, right_side, 0, 0)


def rms_norm(values, gain):
    return values * lax.rsqrt(jnp.mean(values * values, axis=-1, keepdims=True) + epsilon) * gain


def gated_norm(values, gates, gain):
    return rms_norm(values, gain) * jax.nn.silu(gates)


def swiglu(gate_rows, up_rows):
    return jax.nn.silu(gate_rows) * up_rows


def swap_seq(values):
    return lax.ppermute(values, "seq", [(0, 1), (1, 0)])


def in_order(own, other, axis):
    first = lax.axis_index("seq") == 0
    return jnp.where(
        first,
        jnp.concatenate([own, other], axis=axis),
        jnp.concatenate([other, own], axis=axis),
    )


def gather_seq(values, axis):
    if lax.axis_size("seq") == 2:
        return in_order(values, swap_seq(values), axis)
    return lax.all_gather(values, "seq", axis=axis, tiled=True)


def own_part(values, axis, index=None):
    size = values.shape[axis] // lax.axis_size("seq")
    index = lax.axis_index("seq") if index is None else index
    return lax.dynamic_slice_in_dim(values, index * size, size, axis=axis)


def sum_scatter_seq(values, axis):
    if lax.axis_size("seq") == 2:
        other = own_part(values, axis, 1 - lax.axis_index("seq")).astype(bf16)
        return own_part(values, axis) + swap_seq(other).astype(f32)
    return lax.psum_scatter(
        values.astype(bf16), "seq", scatter_dimension=axis, tiled=True
    ).astype(f32)


def sum_seq(values):
    if lax.axis_size("seq") == 2:
        low = values.astype(bf16)
        return low.astype(f32) + swap_seq(low).astype(f32)
    return lax.psum(values.astype(bf16), "seq").astype(f32)


def exchange_seq(values, split, join):
    if lax.axis_size("seq") == 2:
        other = own_part(values, split, 1 - lax.axis_index("seq"))
        return in_order(own_part(values, split), swap_seq(other), join)
    return lax.all_to_all(values, "seq", split_axis=split, concat_axis=join, tiled=True)


def gather_shard(values):
    return lax.all_gather(values, "shard", axis=0, tiled=True)


def scatter_shard(values):
    return lax.psum_scatter(values, "shard", scatter_dimension=0, tiled=True)


def on_device(
    tokens,
    doc_starts,
    norm_gain,
    query_weight,
    key_weight,
    value_weight,
    gate_weight,
    beta_decay_weight,
    conv_filters,
    decay_params,
    out_norm_gain,
    out_weight,
    ffn_norm_gain,
    ffn_gate_weight,
    ffn_up_weight,
    down_weight,
    out_cotangent,
):
    heads = HEADS // lax.axis_size("seq")
    shards = lax.axis_size("shard")
    rows = query_weight.shape[0]
    width = heads * (2 * KEY + VALUE)
    wide = width + KEY
    ff = ffn_gate_weight.shape[1]

    logit_weight = own_part(beta_decay_weight.reshape(rows, HEADS, 2), 1)
    gain_rows = out_norm_gain.shape[0]
    extra = jnp.concatenate(
        [
            logit_weight[:, :, 0],
            logit_weight[:, :, 1],
            norm_gain[:, None],
            ffn_norm_gain[:, None],
            jnp.pad(out_norm_gain, (0, rows - gain_rows))[:, None],
            jnp.zeros((rows, KEY - 2 * heads - 3), bf16),
        ],
        axis=1,
    )
    mixer_piece = jnp.concatenate(
        [
            own_part(query_weight, 1),
            own_part(key_weight, 1),
            own_part(value_weight, 1),
            extra,
            own_part(gate_weight, 1),
        ],
        axis=1,
    )
    mixer_full = gather_shard(mixer_piece)
    out_full = gather_shard(out_weight)
    ffn_full = gather_shard(jnp.concatenate([ffn_gate_weight, ffn_up_weight], axis=1))
    down_full = gather_shard(down_weight)
    raw_full = mixer_full[:, :wide]
    gate_full = mixer_full[:, wide:]
    first_gain = mixer_full[:, width + 2 * heads].astype(f32)
    second_gain = mixer_full[:, width + 2 * heads + 1].astype(f32)
    third_gain = (
        mixer_full[:, width + 2 * heads + 2]
        .reshape(shards, rows)[:, :gain_rows]
        .reshape(shards * gain_rows)
        .astype(f32)
    )

    own_tokens = tokens[0]
    token_count = own_tokens.shape[0]
    inputs = own_tokens.astype(f32)
    all_inputs = gather_seq(own_tokens, 0).astype(f32)
    length = all_inputs.shape[0]
    all_scaled = all_inputs * lax.rsqrt(
        jnp.mean(all_inputs * all_inputs, axis=-1, keepdims=True) + epsilon
    )
    normed = (all_scaled * first_gain).astype(bf16)
    raw = forward_dot(normed, raw_full).astype(bf16)
    gate_rows = forward_dot(normed, gate_full)
    filters = jnp.concatenate(
        [
            conv_filters[:, :, :KEY].reshape(CONV, heads * KEY),
            conv_filters[:, :, KEY : 2 * KEY].reshape(CONV, heads * KEY),
            conv_filters[:, :, 2 * KEY :].reshape(CONV, heads * VALUE),
        ],
        axis=1,
    )
    decays = decay_params.T
    mixed, *kept = mixer_forward(raw, filters, decays, doc_starts, heads)
    gated, gated_pull = jax.vjp(
        gated_norm,
        mixed.astype(f32).reshape(length, heads, VALUE),
        gate_rows.reshape(length, heads, VALUE),
        third_gain,
    )
    gated_low = exchange_seq(gated.astype(bf16).reshape(length, heads * VALUE), 0, 1)
    middle = inputs + forward_dot(gated_low, out_full)
    second_norm, second_pull = jax.vjp(rms_norm, middle, second_gain)
    hidden = second_norm.astype(bf16)
    both_ffn = forward_dot(hidden, ffn_full)
    activated, swiglu_pull = jax.vjp(swiglu, both_ffn[:, :ff], both_ffn[:, ff:])
    activated_low = activated.astype(bf16)
    block_out = (middle + forward_dot(activated_low, down_full)).astype(bf16)

    cotangent = out_cotangent[0]
    act_grad = times_transposed(cotangent, down_full)
    down_grad = transposed_times(activated_low, cotangent).astype(bf16)
    both_grad = jnp.concatenate([g.astype(bf16) for g in swiglu_pull(act_grad)], axis=1)
    ffn_grad = transposed_times(hidden, both_grad).astype(bf16)
    hidden_grad = times_transposed(both_grad, ffn_full)
    middle_part, ffn_gain_grad = second_pull(hidden_grad)
    middle_grad = cotangent.astype(f32) + middle_part
    branch_low = middle_grad.astype(bf16)
    out_grad = transposed_times(gated_low, branch_low).astype(bf16)
    gated_grad = exchange_seq(times_transposed(branch_low, out_full).astype(bf16), 1, 0)
    mixed_grad, gate_rows_grad, out_gain_grad = gated_pull(
        gated_grad.astype(f32).reshape(length, heads, VALUE)
    )
    raw_grad, filters_grad, decays_grad = mixer_backward(
        raw,
        filters,
        decays,
        doc_starts,
        mixed_grad.astype(bf16).reshape(length, heads * VALUE),
        kept,
        heads,
    )
    gate_low = gate_rows_grad.astype(bf16).reshape(length, heads * VALUE)
    normed_grad = times_transposed(raw_grad, raw_full) + times_transposed(gate_low, gate_full)
    raw_weight_grad = transposed_times(normed, raw_grad).astype(bf16)
    gate_weight_grad = transposed_times(normed, gate_low).astype(bf16)
    norm_gain_grad = jnp.sum(normed_grad * all_scaled, axis=0)
    own_normed_grad = sum_scatter_seq(normed_grad, 0)
    _, first_pull = jax.vjp(lambda v: rms_norm(v, first_gain), inputs)
    tokens_grad = middle_grad + first_pull(own_normed_grad)[0]

    down_share = sum_seq(scatter_shard(down_grad))
    ffn_share = sum_seq(scatter_shard(ffn_grad))
    out_share = sum_seq(scatter_shard(out_grad))
    gate_share = gather_seq(scatter_shard(gate_weight_grad), 1).astype(f32)
    raw_share = scatter_shard(raw_weight_grad)
    query_share = gather_seq(raw_share[:, : heads * KEY], 1).astype(f32)
    key_share = gather_seq(raw_share[:, heads * KEY : 2 * heads * KEY], 1).astype(f32)
    value_share = gather_seq(raw_share[:, 2 * heads * KEY : width], 1).astype(f32)
    logit_share = jnp.stack(
        [
            raw_share[:, width : width + heads],
            raw_share[:, width + heads : width + 2 * heads],
        ],
        axis=2,
    ).reshape(rows, 2 * heads)
    logit_share = gather_seq(logit_share, 1).astype(f32)

    filters_grad = jnp.sum(filters_grad.reshape(CONV, 8, width), axis=1)
    filters_grad, decays_grad = lax.psum((filters_grad, decays_grad), "shard")
    split = (heads * KEY, 2 * heads * KEY)
    filters_out = jnp.concatenate(
        [
            filters_grad[:, : split[0]].reshape(CONV, heads, KEY),
            filters_grad[:, split[0] : split[1]].reshape(CONV, heads, KEY),
            filters_grad[:, split[1] :].reshape(CONV, heads, VALUE),
        ],
        axis=2,
    )
    gains = lax.psum((norm_gain_grad, out_gain_grad, ffn_gain_grad), ("seq", "shard"))
    place = lax.axis_index("shard")
    gains = [
        lax.dynamic_slice_in_dim(g, place * (g.shape[0] // shards), g.shape[0] // shards)
        for g in gains
    ]
    return (
        block_out[None],
        tokens_grad[None],
        gains[0],
        query_share,
        key_share,
        value_share,
        gate_share,
        logit_share,
        filters_out,
        decays_grad.T,
        gains[1],
        out_share,
        gains[2],
        ffn_share[:, :ff],
        ffn_share[:, ff:],
        down_share,
    )


def solution(mesh):
    in_specs = (
        P("shard", "seq", None),
        P("shard", None),
        P("shard"),
        P("shard", None),
        P("shard", None),
        P("shard", None),
        P("shard", None),
        P("shard", None),
        P(None, "seq", None),
        P("seq", None),
        P("shard"),
        P("shard", None),
        P("shard"),
        P("shard", None),
        P("shard", None),
        P("shard", None),
        P("shard", "seq", None),
    )
    out_specs = (
        P("shard", "seq", None),
        P("shard", "seq", None),
        P("shard"),
        P("shard", None),
        P("shard", None),
        P("shard", None),
        P("shard", None),
        P("shard", None),
        P(None, "seq", None),
        P("seq", None),
        P("shard"),
        P("shard", None),
        P("shard"),
        P("shard", None),
        P("shard", None),
        P("shard", None),
    )
    return jax.shard_map(
        on_device, mesh=mesh, in_specs=in_specs, out_specs=out_specs, check_vma=False
    )
```

time: 2110 us -> 829 us (0.39)
  other arithmetic: 503 us -> 43.9 us
  matrix products: 445 us -> 125 us
  waiting for transfers between devices: 625 us -> 381 us
  local copies, waits for them, and re-layouts: 277 us -> 52.9 us
  Pallas kernels: 0 us -> 93.7 us
  blocking collectives: 186 us -> 97.9 us
    another operation x25 -> x1, other arithmetic: 349 us -> 0.01 us  [on_device(): jnp.stack([raw_share[:, width:width + heads], raw_share[:, width + heads:...]
    dot_general x242 -> x15, matrix products: 424 us -> 125 us  [the longest x10 82.4 us: dot(): lax.dot_general(a, b, (((ca,), (cb,)), ((), ())), preferred_element_type=...]
    reduce_scatter x8 -> x5, waiting for transfers between devices: 484 us -> 196 us  [scatter_shard(): return lax.psum_scatter(values, 'shard', scatter_dimension=0, tiled=True)]
    squeeze x97 -> x0, local copies, waits for them, and re-layouts: 101 us -> none  [the longest x96 101 us: delta_rule(): lax.scan(jax.checkpoint(advance), start, (new_values, corrections, scores...]
    pallas_call x0 -> x2, Pallas kernels: none -> 93.7 us  [the longest x1 51.7 us: mixer_backward(): pl.pallas_call(functools.partial(backward_kernel, heads), grid=(steps,),...]
    ppermute x0 -> x12, waiting for transfers between devices: none -> 75.2 us  [swap_seq(): return lax.ppermute(values, 'seq', [(0, 1), (1, 0)])]
    unnamed x2 -> x0, blocking collectives: 67.9 us -> none
    all_to_all x8 -> x0, waiting for transfers between devices: 65 us -> none  [the longest x1 21.2 us: on_device(): lax.all_to_all(value_raw.reshape(token_count, HEADS, VALUE), 'seq', split...]
  transfers between devices with their start and end apart: 26 -> 21, of which waited for: 14 -> 11; matrix products, arithmetic and copies ran while one was open for 34% -> 19% of each run, Pallas kernels for 0% -> 11%
where the time goes in v1:
time: 829 us; the launch traced here: 826 us
  waiting for transfers between devices  381 us (46%)
  matrix products  125 us (15%)
  blocking collectives  97.9 us (12%)
  Pallas kernels  93.7 us (11%)
  local copies, waits for them, and re-layouts  52.9 us (6%)
  other arithmetic  43.9 us (5%)
  starting transfers between devices  17.5 us (2%)
  between operations  14.5 us (2%)
    reduce_scatter x5, waiting for transfers between devices, scatter_shard(): return lax.psum_scatter(values, 'shard', scatter_dimension=0, tiled=True)  196 us
    all_gather x4, waiting for transfers between devices, gather_shard(): return lax.all_gather(values, 'shard', axis=0, tiled=True)  108 us
    dot_general x10, matrix products, dot(): lax.dot_general(a, b, (((ca,), (cb,)), ((), ())), preferred_element_type=...  82.4 us
    ppermute x12, waiting for transfers between devices, swap_seq(): return lax.ppermute(values, 'seq', [(0, 1), (1, 0)])  75.2 us
    psum x1, blocking collectives, on_device(): filters_grad, decays_grad = lax.psum((filters_grad, decays_grad), 'shard')  59.2 us
    pallas_call x1, Pallas kernels, mixer_backward(): pl.pallas_call(functools.partial(backward_kernel, heads), grid=(steps,),...  51.7 us
    dot_general x5, matrix products, forward_dot(): return jnp.dot(left_side, right_side, preferred_element_type=f32)  42.6 us
    pallas_call x1, Pallas kernels, mixer_forward(): pl.pallas_call(functools.partial(forward_kernel, heads), grid=(steps,), i...  42 us
  transfers between devices with their start and end apart: 21, of which 11 were waited for; matrix products, arithmetic and copies ran while one was open for 19% of the time, Pallas kernels for 11%

profile of v1, /device:TPU:0, one launch (start us, length us, event | category | flops | bytes accessed | tf_op | source)
XLA Modules:
  0.0 826.0 jit_solution(6995295570746731932)
XLA Ops:
  14.2 2.0 pad_maximum_fusion.3
  16.8 3.0 collective-permute-start
  19.9 23.1 %collective-permute-done = bf16[512,1024]{1,0:T(8,128)(2,1)S(1)} collective-permute-done((bf16[512,1024]{1,0:T(8,128)(2,1)S(1)}, bf16[512,1024]{1,0:T(8,128)(2,1)S(1)}, u32[]{:S(2)}, u32[]{:S(2)}) %collective-permute-start) | collective-permute-done | bytes 1048608 | tf_op jit(solution)/shard_map/ppermute | solution.py:546
  43.7 35.9 %all-gather.5.cloned.1.call-done = bf16[1024,3200]{1,0:T(8,128)(2,1)} async-done(((bf16[64,3200]{1,0:T(8,128)(2,1)}), bf16[1024,3200]{1,0:T(8,128)(2,1)}) %all-gather.5.cloned.1.call-update) | async-done | bytes 6553616 | tf_op jit(solution)/shard_map/all_gather | solution.py:594
  82.4 11.2 %convolution_convert_fusion.3.raw_ref = bf16[1024,2176]{1,0:T(8,128)(2,1)} fusion(bf16[1024,3200]{1,0:T(8,128)(2,1)} %all-gather.5.cloned.1.call-done, f32[1024]{0:T(1024)S(1)} %get-tuple-element.33, f32[1024]{0:T(1024)S(1)} %add_rsqrt_fusion, bf16[512,1024]{1,0:T(8,128)(2,1)S(1)} %bitcast.83, bf16[512,1024]{1,0:T(8,128)(2,1)S(1)} %collective-permute-done, ...), kind=kOutput, calls=%fused_computation.14 | convolution fusion | flops 4579262464 | bytes 11018241 | tf_op jit(solution)/shard_map/dot_general | solution.py:522
  93.6 42.0 %mixer_forward.1 = (bf16[1024,1024]{1,0:T(8,128)(2,1)}, bf16[1024,256]{1,0:T(8,128)(2,1)}, bf16[4096,256]{1,0:T(8,128)(2,1)}, bf16[4096,256]{1,0:T(8,128)(2,1)}, bf16[8192,256]{1,0:T(8,128)(2,1)}) custom-call(s32[1,4]{1,0:T(1,128)} %starts_ref.3, bf16[1024,2176]{1,0:T(8,128)(2,1)} %convolution_convert_fusion.3.raw_ref, f32[4,2048]{1,0:T(4,128)} %copy-done.18, ...), custom_call_target="tpu_custom_call" | custom-call | tf_op jit(solution)/shard_map/mixer_forward/pallas_call | solution.py:465
  135.6 5.1 reshape.194
  140.7 3.7 multiply_reduce_fusion.1
  146.2 3.0 copy.132
  149.2 7.7 fusion.26
  156.9 5.5 copy.112
  162.5 4.8 multiply_convert_fusion.2
  170.3 24.1 %collective-permute-done.1 = bf16[512,1024]{1,0:T(8,128)(2,1)} collective-permute-done((bf16[512,1024]{1,0:T(8,128)(2,1)}, bf16[512,1024]{1,0:T(8,128)(2,1)}, u32[]{:S(2)}, u32[]{:S(2)}) %collective-permute-start.1) | collective-permute-done | bytes 1048608 | tf_op jit(solution)/shard_map/ppermute | solution.py:546
  194.5 7.2 multiply_reduce_fusion.4
  201.7 25.5 %all-gather.9.cloned.1.call-done = bf16[1024,5632]{1,0:T(8,128)(2,1)} async-done(((bf16[64,5632]{1,0:T(8,128)(2,1)}), bf16[1024,5632]{1,0:T(8,128)(2,1)}) %all-gather.9.cloned.1.call-update) | async-done | bytes 11534352 | tf_op jit(solution)/shard_map/all_gather | solution.py:594
  227.2 12.4 %fusion.46 = f32[512,5632]{1,0:T(8,128)} fusion(bf16[1024,5632]{1,0:T(8,128)(2,1)} %all-gather.9.cloned.1.call-done, f32[512,1024]{1,0:T(8,128)} %get-tuple-element.70, f32[1024]{0:T(1024)S(1)} %get-tuple-element.32, f32[512]{0:T(512)S(1)} %fusion.40), kind=kOutput, calls=%fused_computation.131 | convolution fusion | flops 5907152896 | bytes 25171968 | tf_op jit(solution)/shard_map/dot_general | solution.py:522
  239.6 47.0 %all-gather.11.cloned.1.call-done = bf16[2816,1024]{1,0:T(8,128)(2,1)} async-done(((bf16[176,1024]{1,0:T(8,128)(2,1)}), bf16[2816,1024]{1,0:T(8,128)(2,1)}) %all-gather.11.cloned.1.call-update) | async-done | bytes 5767184 | tf_op jit(solution)/shard_map/all_gather | solution.py:594
  286.6 12.9 %fusion.2 = (bf16[512,2816]{1,0:T(8,128)(2,1)}, bf16[512,2816]{1,0:T(8,128)(2,1)}, bf16[512,2816]{1,0:T(8,128)(2,1)}) fusion(f32[512,5632]{1,0:T(8,128)} %fusion.46, bf16[2816,1024]{1,0:T(8,128)(2,1)} %all-gather.11.cloned.1.call-done, bf16[1,512,1024]{2,1,0:T(8,128)(2,1)} %param.33), kind=kOutput, calls=%fused_computation.6 | convolution fusion | flops 2975858688 | bytes 27000832 | tf_op jit(solution)/shard_map/dot_general | solution.py:23
  299.5 12.8 %multiply_reduce_fusion.2 = (f32[1024]{0:T(1024)S(1)}, f32[512]{0:T(512)S(1)}, f32[512,1024]{1,0:T(8,128)}) fusion(f32[512,1024]{1,0:T(8,128)S(1)} %copy-done.8, f32[512]{0:T(512)S(1)} %fusion.40, f32[1024]{0:T(1024)S(1)} %get-tuple-element.32, bf16[1024,5632]{1,0:T(8,128)(2,1)} %all-gather.9.cloned.1.call-done, bf16[512,2816]{1,0:T(8,128)(2,1)} %get-tuple-element.46, ...), kind=kOutput, calls=%fused_computation.56 | convolution fusion | flops 5920258560 | bytes 21508096 | tf_op jit(solution)/shard_map/dot_general | solution.py:23
  312.3 2.3 fusion.19
  315.1 2.4 convolution_convert_fusion.5
  320.5 2.4 convert_element_type.152
  322.9 5.4 copy.119
  328.3 2.3 copy.113
  330.6 2.3 copy.114
  332.9 11.8 %collective-permute-done.2 = bf16[512,1024]{1,0:T(8,128)(2,1)} collective-permute-done((bf16[512,1024]{1,0:T(8,128)(2,1)}, bf16[512,1024]{1,0:T(8,128)(2,1)}, u32[]{:S(2)}, u32[]{:S(2)}) %collective-permute-start.2) | collective-permute-done | bytes 1048608 | tf_op jit(solution)/shard_map/ppermute | solution.py:546
  345.9 4.9 fusion.13
  351.9 2.3 broadcast_in_dim.43
  357.6 6.4 fusion.12
  365.4 4.0 convolution_convert_fusion.6
  369.5 6.7 convolution_convert_fusion.4
  376.2 51.7 %mixer_backward.1 = (bf16[1024,2176]{1,0:T(8,128)(2,1)}, f32[32,2048]{1,0:T(8,128)}, f32[2,4]{1,0:T(2,128)}) custom-call(s32[1,4]{1,0:T(1,128)} %starts_ref.3, bf16[1024,2176]{1,0:T(8,128)(2,1)} %convolution_convert_fusion.3.raw_ref, f32[4,2048]{1,0:T(4,128)} %copy-done.18, f32[2,4]{1,0:T(2,128)} %bitcast.99, ...), custom_call_target="tpu_custom_call" | custom-call | tf_op jit(solution)/shard_map/mixer_backward/pallas_call | solution.py:494
  428.0 10.0 %convolution_convert_fusion.2 = bf16[1024,2176]{1,0:T(8,128)(2,1)} fusion(bf16[1024,2176]{1,0:T(8,128)(2,1)} %get-tuple-element.29, f32[1024]{0:T(1024)S(1)} %get-tuple-element.33, f32[1024]{0:T(1024)S(1)} %add_rsqrt_fusion, bf16[512,1024]{1,0:T(8,128)(2,1)S(1)} %bitcast.86, bf16[512,1024]{1,0:T(8,128)(2,1)S(1)} %copy-done.13, pred[]{:T(512)S(6)} %eq.2), kind=kOutput, calls=%fused_computation.13 | convolution fusion | flops 4579262464 | bytes 11018241 | tf_op jit(solution)/shard_map/dot_general | solution.py:23
  438.0 7.8 convolution_convert_fusion.1
  445.9 12.4 %convolution_convert_fusion = bf16[1024,5632]{1,0:T(8,128)(2,1)} fusion(bf16[512,2816]{1,0:T(8,128)(2,1)} %get-tuple-element.46, bf16[512,2816]{1,0:T(8,128)(2,1)} %get-tuple-element.45, f32[512,1024]{1,0:T(8,128)} %get-tuple-element.70, f32[1024]{0:T(1024)S(1)} %get-tuple-element.32, f32[512]{0:T(512)S(1)} %fusion.40), kind=kOutput, calls=%fused_computation | convolution fusion | flops 5924454400 | bytes 19404800 | tf_op jit(solution)/shard_map/dot_general | solution.py:23
  458.4 4.7 fusion.24
  463.1 8.7 %fusion.7 = (f32[1024]{0:T(1024)S(1)}, f32[1024,1024]{1,0:T(8,128)S(1)}) fusion(f32[1024]{0:T(1024)S(1)} %add_rsqrt_fusion, bf16[512,1024]{1,0:T(8,128)(2,1)S(1)} %bitcast.87, bf16[512,1024]{1,0:T(8,128)(2,1)S(1)} %copy-done.14, pred[]{:T(512)S(6)} %eq.2, f32[1024,1024]{1,0:T(8,128)S(1)} %fusion.24, bf16[1024,2176]{1,0:T(8,128)(2,1)} %get-tuple-element.29, ...), kind=kOutput, calls=%fused_computation.22 | convolution fusion | flops 4578081792 | bytes 19406848 | tf_op jit(solution)/shard_map/dot_general | solution.py:23
  474.8 4.1 fusion.28
  479.0 59.2 %all-reduce.2 = (f32[4,2048]{1,0:T(4,128)S(1)}, f32[4,2]{0,1:T(2,128)}) all-reduce(f32[4,2048]{1,0:T(4,128)S(1)} %bitcast_reduce_fusion, f32[4,2]{0,1:T(2,128)S(1)} %bitcast.100), channel_id=1, replica_groups=mesh['seq'=2,'shard'=16] {'shard'}, use_global_device_ids=true, to_apply=%region_12.13 | all-reduce | flops 8200 | bytes 65600 | tf_op jit(solution)/shard_map/psum | solution.py:751
  538.3 38.6 %all-reduce.1 = (f32[1024]{0:T(1024)S(1)}, f32[256]{0:T(256)S(1)}, f32[1024]{0:T(1024)S(1)}) all-reduce(f32[1024]{0:T(1024)S(1)} %get-tuple-element.43, f32[256]{0:T(256)S(1)} %reduce_sum.137, f32[1024]{0:T(1024)S(1)} %get-tuple-element.34), channel_id=1, replica_groups=mesh['seq'=2,'shard'=16] {'seq','shard'}, use_global_device_ids=true, to_apply=%region_8.9 | all-reduce | flops 2304 | bytes 18432 | tf_op jit(solution)/shard_map/psum | solution.py:761
  579.3 2.6 fusion.22
  581.9 2.3 collective-permute-start.7
  584.4 3.9 fusion.21
  589.8 3.4 collective-permute-done.9
  601.6 67.1 %reduce-scatter.14.cloned.1.call-done = bf16[176,1024]{1,0:T(8,128)(2,1)} async-done(((bf16[2816,1024]{1,0:T(8,128)(2,1)}), bf16[176,1024]{1,0:T(8,128)(2,1)}) %reduce-scatter.14.cloned.1.call-update) | async-done | bytes 360464 | tf_op jit(solution)/shard_map/reduce_scatter | solution.py:598
  670.3 128.6 %reduce-scatter.12.cloned.1.call-done = bf16[64,5632]{1,0:T(8,128)(2,1)} async-done(((bf16[1024,5632]{1,0:T(8,128)(2,1)}), bf16[64,5632]{1,0:T(8,128)(2,1)}) %reduce-scatter.12.cloned.1.call-update) | async-done | bytes 720912 | tf_op jit(solution)/shard_map/reduce_scatter | solution.py:598
  802.7 1.9 convert_add_fusion.2
  804.6 12.2 %collective-permute-done.10 = bf16[64,5632]{1,0:T(8,128)(2,1)S(1)} collective-permute-done((bf16[64,5632]{1,0:T(8,128)(2,1)}, bf16[64,5632]{1,0:T(8,128)(2,1)S(1)}, u32[]{:S(2)}, u32[]{:S(2)}) %collective-permute-start.10) | collective-permute-done | bytes 720928 | tf_op jit(solution)/shard_map/ppermute | solution.py:546
  (157 shorter events, 50.1 us)
Async XLA Ops:
  7.2 9.6 %copy-start.3 = (bf16[1,512,1024]{2,1,0:T(8,128)(2,1)S(1)}, bf16[1,512,1024]{2,1,0:T(8,128)(2,1)}, u32[]{:S(2)}) copy-start(bf16[1,512,1024]{2,1,0:T(8,128)(2,1)} %param.17) | copy-start | bytes 3145732
  7.2 12.6 %copy-start.20 = (f32[4,4,512]{2,1,0:T(4,128)S(1)}, f32[4,4,512]{2,1,0:T(4,128)}, u32[]{:S(2)}) copy-start(f32[4,4,512]{2,1,0:T(4,128)} %param.25) | copy-start | bytes 98308
  7.2 72.4 %all-gather.5.cloned.1.call-start = ((), (), s32[]{:S(2)}) async-start(), calls=%async_computation.5 | async-start | bytes 6963200 | tf_op jit(solution)/shard_map/all_gather | solution.py:594
  13.4 157.0 %all-gather.7.cloned.1.call-start = ((), (), s32[]{:S(2)}) async-start(), calls=%async_computation.6 | async-start | bytes 4456448 | tf_op jit(solution)/shard_map/all_gather | solution.py:594
  14.1 213.1 %all-gather.9.cloned.1.call-start = ((), (), s32[]{:S(2)}) async-start(), calls=%async_computation.7 | async-start | bytes 12255232 | tf_op jit(solution)/shard_map/all_gather | solution.py:594
  16.2 270.4 %all-gather.11.cloned.1.call-start = ((), (), s32[]{:S(2)}) async-start(), calls=%async_computation.8 | async-start | bytes 6127616 | tf_op jit(solution)/shard_map/all_gather | solution.py:594
  16.8 565.2 %reduce-scatter.8.cloned.1.call-start = ((), (), s32[]{:S(2)}) async-start(), calls=%async_computation.10 | async-start | bytes 2228224 | tf_op jit(solution)/shard_map/reduce_scatter | solution.py:598
  16.8 26.2 %collective-permute-start = (bf16[512,1024]{1,0:T(8,128)(2,1)S(1)}, bf16[512,1024]{1,0:T(8,128)(2,1)S(1)}, u32[]{:S(2)}, u32[]{:S(2)}) collective-permute-start(bf16[512,1024]{1,0:T(8,128)(2,1)S(1)} %bitcast.81), channel_id=1, source_target_pairs={{0,16},{16,0},{1,17},{17,1},{2,18},{18,2},{3,19},{19,3},{4,20},{20... | collective-permute-start | bytes 3145736 | tf_op jit(solution)/shard_map/ppermute | solution.py:546
  19.9 73.7 %copy-start.18 = (f32[4,2048]{1,0:T(4,128)}, f32[4,2048]{1,0:T(4,128)S(1)}, u32[]{:S(2)}) copy-start(f32[4,2048]{1,0:T(4,128)S(1)} %constant_dynamic-update-slice_fusion.filters_ref) | copy-start | bytes 98308
  43.0 106.2 %copy-start.11 = (bf16[512,1024]{1,0:T(8,128)(2,1)}, bf16[512,1024]{1,0:T(8,128)(2,1)S(1)}, u32[]{:S(2)}) copy-start(bf16[512,1024]{1,0:T(8,128)(2,1)S(1)} %collective-permute-done) | copy-start | bytes 3145732
  156.9 5.5 copy-start.2
  168.8 25.7 %collective-permute-start.1 = (bf16[512,1024]{1,0:T(8,128)(2,1)}, bf16[512,1024]{1,0:T(8,128)(2,1)}, u32[]{:S(2)}, u32[]{:S(2)}) collective-permute-start(bf16[512,1024]{1,0:T(8,128)(2,1)} %get-tuple-element.54), channel_id=1, source_target_pairs={{0,16},{16,0},{1,17},{17,1},{2,18},{18,2},{3,19},{19,3},{4,20},{20... | collective-permute-start | bytes 3145736 | tf_op jit(solution)/shard_map/ppermute | solution.py:546
  286.6 12.9 %copy-start.8 = (f32[512,1024]{1,0:T(8,128)S(1)}, f32[512,1024]{1,0:T(8,128)}, u32[]{:S(2)}) copy-start(f32[512,1024]{1,0:T(8,128)} %get-tuple-element.70) | copy-start | bytes 6291460
  299.5 12.8 %copy-start.15 = (bf16[1,512,1024]{2,1,0:T(8,128)(2,1)S(1)}, bf16[1,512,1024]{2,1,0:T(8,128)(2,1)}, u32[]{:S(2)}) copy-start(bf16[1,512,1024]{2,1,0:T(8,128)(2,1)} %param.33) | copy-start | bytes 3145732
  312.3 2.8 copy-start.22
  315.1 2.4 copy-start.5
  319.0 25.6 %collective-permute-start.2 = (bf16[512,1024]{1,0:T(8,128)(2,1)}, bf16[512,1024]{1,0:T(8,128)(2,1)}, u32[]{:S(2)}, u32[]{:S(2)}) collective-permute-start(bf16[512,1024]{1,0:T(8,128)(2,1)} %get-tuple-element.52), channel_id=1, source_target_pairs={{0,16},{16,0},{1,17},{17,1},{2,18},{18,2},{3,19},{19,3},{4,20},{20... | collective-permute-start | bytes 3145736 | tf_op jit(solution)/shard_map/ppermute | solution.py:546
  351.9 3.4 copy-start.4
  354.2 2.2 copy-start
  354.2 3.5 copy-start.1
  357.6 7.7 copy-start.12
  364.1 1.3 copy-start.10
  365.4 4.1 copy-start.6
  369.4 214.9 %reduce-scatter.10.cloned.1.call-start = ((), (), s32[]{:S(2)}) async-start(), calls=%async_computation.11 | async-start | bytes 4456448 | tf_op jit(solution)/shard_map/reduce_scatter | solution.py:598
  376.2 217.8 %reduce-scatter.6.cloned.1.call-start = ((), (), s32[]{:S(2)}) async-start(), calls=%async_computation.9 | async-start | bytes 4734976 | tf_op jit(solution)/shard_map/reduce_scatter | solution.py:598
  376.2 51.8 %copy-start.13 = (bf16[512,1024]{1,0:T(8,128)(2,1)S(1)}, bf16[512,1024]{1,0:T(8,128)(2,1)}, u32[]{:S(2)}) copy-start(bf16[512,1024]{1,0:T(8,128)(2,1)} %copy-done.11) | copy-start | bytes 3145732
  437.9 230.8 %reduce-scatter.14.cloned.1.call-start = ((), (), s32[]{:S(2)}) async-start(), calls=%async_computation.13 | async-start | bytes 6127616 | tf_op jit(solution)/shard_map/reduce_scatter | solution.py:598
  445.8 353.0 %reduce-scatter.12.cloned.1.call-start = ((), (), s32[]{:S(2)}) async-start(), calls=%async_computation.12 | async-start | bytes 12255232 | tf_op jit(solution)/shard_map/reduce_scatter | solution.py:598
  458.3 4.8 copy-start.14
  458.4 16.4 %slice-start = ((s8[5767168]{0:T(1024)(128)(4,1)}), s8[4194304]{0:T(1024)(128)(4,1)S(1)}, s32[]{:S(2)}) async-start(s8[5767168]{0:T(1024)(128)(4,1)} %bitcast.103), calls=%async_computation.14 | async-start | bytes 8388608
  463.1 11.7 %copy-start.9 = (f32[512,1024]{1,0:T(8,128)S(1)}, f32[512,1024]{1,0:T(8,128)}, u32[]{:S(2)}) copy-start(f32[512,1024]{1,0:T(8,128)} %get-tuple-element.70) | copy-start | bytes 6291460
  463.1 11.7 %slice-start.1 = ((s8[5767168]{0:T(1024)(128)(4,1)}), s8[1572864]{0:T(1024)(128)(4,1)S(1)}, s32[]{:S(2)}) async-start(s8[5767168]{0:T(1024)(128)(4,1)} %bitcast.103), calls=%async_computation.15 | async-start | bytes 3145728
  463.1 11.7 %copy-start.23 = (bf16[512,2816]{1,0:T(8,128)(2,1)S(1)}, bf16[512,2816]{1,0:T(8,128)(2,1)}, u32[]{:S(2)}) copy-start(bf16[512,2816]{1,0:T(8,128)(2,1)} %get-tuple-element.50) | copy-start | bytes 8650756
  471.9 7.0 copy-start.7
  473.2 5.7 copy-start.16
  473.2 5.8 copy-start.21
  473.2 106.1 %collective-permute-start.3 = (bf16[512,1024]{1,0:T(8,128)(2,1)}, bf16[512,1024]{1,0:T(8,128)(2,1)}, u32[]{:S(2)}, u32[]{:S(2)}) collective-permute-start(bf16[512,1024]{1,0:T(8,128)(2,1)} %dynamic-slice_convert_fusion), channel_id=1, source_target_pairs={{0,16},{16,0},{1,17},{17,1},{2,18},{18,2},{3,19},{19,3},{4,20},{20... | collective-permute-start | bytes 3145736 | tf_op jit(solution)/shard_map/ppermute | solution.py:546
  581.9 6.9 collective-permute-start.7
  584.3 8.8 %collective-permute-start.9 = (bf16[128,1024]{1,0:T(8,128)(2,1)}, bf16[128,1024]{1,0:T(8,128)(2,1)S(1)}, u32[]{:S(2)}, u32[]{:S(2)}) collective-permute-start(bf16[128,1024]{1,0:T(8,128)(2,1)} %reduce-scatter.10.cloned.1.call-done), channel_id=1, source_target_pairs={{0,16},{16,0},{1,17},{17,1},{2,18},{18,2},{3,19},{19,3},{4,20},{20... | collective-permute-start | bytes 786440 | tf_op jit(solution)/shard_map/ppermute | solution.py:546
  584.4 4.5 copy-start.19
  584.4 8.7 %copy-start.17 = (bf16[128,1024]{1,0:T(8,128)(2,1)S(1)}, bf16[128,1024]{1,0:T(8,128)(2,1)}, u32[]{:S(2)}) copy-start(bf16[128,1024]{1,0:T(8,128)(2,1)} %reduce-scatter.10.cloned.1.call-done) | copy-start | bytes 786436
  595.0 6.0 collective-permute-start.8
  597.2 203.2 %collective-permute-start.4 = (bf16[64,512]{1,0:T(8,128)(2,1)S(1)}, bf16[64,512]{1,0:T(8,128)(2,1)S(1)}, u32[]{:S(2)}, u32[]{:S(2)}) collective-permute-start(bf16[64,512]{1,0:T(8,128)(2,1)S(1)} %get-tuple-element.60), channel_id=1, source_target_pairs={{0,16},{16,0},{1,17},{17,1},{2,18},{18,2},{3,19},{19,3},{4,20},{20... | collective-permute-start | bytes 196616 | tf_op jit(solution)/shard_map/ppermute | solution.py:546
  598.0 203.1 %collective-permute-start.5 = (bf16[64,512]{1,0:T(8,128)(2,1)S(1)}, bf16[64,512]{1,0:T(8,128)(2,1)S(1)}, u32[]{:S(2)}, u32[]{:S(2)}) collective-permute-start(bf16[64,512]{1,0:T(8,128)(2,1)S(1)} %get-tuple-element.59), channel_id=1, source_target_pairs={{0,16},{16,0},{1,17},{17,1},{2,18},{18,2},{3,19},{19,3},{4,20},{20... | collective-permute-start | bytes 196616 | tf_op jit(solution)/shard_map/ppermute | solution.py:546
  600.3 201.6 %collective-permute-start.6 = (bf16[64,1024]{1,0:T(8,128)(2,1)S(1)}, bf16[64,1024]{1,0:T(8,128)(2,1)S(1)}, u32[]{:S(2)}, u32[]{:S(2)}) collective-permute-start(bf16[64,1024]{1,0:T(8,128)(2,1)S(1)} %slice.102), channel_id=1, source_target_pairs={{0,16},{16,0},{1,17},{17,1},{2,18},{18,2},{3,19},{19,3},{4,20},{20... | collective-permute-start | bytes 393224 | tf_op jit(solution)/shard_map/ppermute | solution.py:546
  668.8 133.9 %collective-permute-start.11 = (bf16[176,1024]{1,0:T(8,128)(2,1)}, bf16[176,1024]{1,0:T(8,128)(2,1)S(1)}, u32[]{:S(2)}, u32[]{:S(2)}) collective-permute-start(bf16[176,1024]{1,0:T(8,128)(2,1)} %reduce-scatter.14.cloned.1.call-done), channel_id=1, source_target_pairs={{0,16},{16,0},{1,17},{17,1},{2,18},{18,2},{3,19},{19,3},{4,20},{20... | collective-permute-start | bytes 1081352 | tf_op jit(solution)/shard_map/ppermute | solution.py:546
  798.9 18.0 %collective-permute-start.10 = (bf16[64,5632]{1,0:T(8,128)(2,1)}, bf16[64,5632]{1,0:T(8,128)(2,1)S(1)}, u32[]{:S(2)}, u32[]{:S(2)}) collective-permute-start(bf16[64,5632]{1,0:T(8,128)(2,1)} %reduce-scatter.12.cloned.1.call-done), channel_id=1, source_target_pairs={{0,16},{16,0},{1,17},{17,1},{2,18},{18,2},{3,19},{19,3},{4,20},{20... | collective-permute-start | bytes 2162696 | tf_op jit(solution)/shard_map/ppermute | solution.py:546
Sparse Core Ops, SparseCore 0:
  13.5 66.0 all-gather.4
  81.8 49.6 all-gather.6
  134.3 92.8 all-gather.8
  229.3 57.1 all-gather.10
  369.5 60.1 reduce-scatter.7
  433.9 71.8 reduce-scatter.9
  509.6 73.9 reduce-scatter.5
  588.1 80.6 reduce-scatter.13
  673.4 125.3 reduce-scatter.11

commit v2 on v1

--- a/solution.py
+++ b/solution.py
@@ -125,9 +125,9 @@
 
 
 class Block:
-    def __init__(self, heads, base, raw_ref, filters_ref, decay_ref, starts_ref, backward=False):
+    def __init__(self, heads, base, raw_ref, value_ref, filters_ref, decay_ref, starts_ref):
         self.heads = heads
-        width = heads * (2 * KEY + VALUE)
+        width = 2 * heads * KEY
         times = base + iota((GROUP, 1), 0)
         docs = doc_count(starts_ref, times)
         self.masks = [
@@ -135,6 +135,7 @@
         ]
         self.base = base
         self.raw_ref = raw_ref
+        self.value_ref = value_ref
         self.filters_ref = filters_ref
         self.query, self.keys, self.query_pre, self.key_pre = [], [], [], []
         self.query_conv, self.key_conv, self.query_scale, self.key_scale = [], [], [], []
@@ -154,7 +155,7 @@
             self.key_conv.append(conv)
             self.key_scale.append(scale)
             self.keys.append(conv * scale)
-        logits = raw_ref[pl.ds(base, GROUP), width : width + 2 * KEY // 2].astype(f32)
+        logits = raw_ref[pl.ds(base, GROUP), width : width + KEY].astype(f32)
         self.strength = sigmoid(logits[:, :heads])
         self.decay_logit = logits[:, heads : 2 * heads] + decay_ref[1:2, :heads]
         self.decay_rate = -jnp.exp(decay_ref[0:1, :heads])
@@ -197,9 +198,13 @@
         self.scores = self.score_gram * self.fade
 
     def taps(self, start, width):
-        current = self.raw_ref[pl.ds(self.base, GROUP), start : start + width].astype(f32)
+        source = self.raw_ref
+        if start >= 2 * self.heads * KEY:
+            source = self.value_ref
+            start = start - 2 * self.heads * KEY
+        current = source[pl.ds(self.base, GROUP), start : start + width].astype(f32)
         earlier = pl.multiple_of(jnp.maximum(self.base - HALO, 0), HALO)
-        halo = self.raw_ref[pl.ds(earlier, HALO), start : start + width].astype(f32)
+        halo = source[pl.ds(earlier, HALO), start : start + width].astype(f32)
         extended = jnp.concatenate([halo, current], axis=0)
         return [current] + [
             pltpu.roll(extended, o, 0)[HALO:] * self.masks[o - 1] for o in range(1, CONV)
@@ -232,8 +237,8 @@
 
 
 def forward_kernel(
-    heads, starts_ref, raw_ref, filters_ref, decay_ref,
-    mixed_ref, inverse_ref, delta_ref, rest_ref, memory_ref, state,
+    heads, starts_ref, raw_ref, value_ref, filters_ref, decay_ref, gate_ref, gain_ref,
+    gated_ref, mixed_ref, inverse_ref, delta_ref, rest_ref, memory_ref, state,
 ):
     step = pl.program_id(0)
 
@@ -244,7 +249,7 @@
     blocks = []
     for s in range(SUB):
         base = pl.multiple_of((step * SUB + s) * GROUP, GROUP)
-        block = Block(heads, base, raw_ref, filters_ref, decay_ref, starts_ref)
+        block = Block(heads, base, raw_ref, value_ref, filters_ref, decay_ref, starts_ref)
         block.values = []
         for h in range(heads):
             pre = block.convolve(2 * heads * KEY + h * VALUE, VALUE)
@@ -271,7 +276,15 @@
         for h in range(heads):
             rows = slice(h * GROUP, (h + 1) * GROUP)
             out = from_state[h] + outputs[rows]
-            mixed_ref[s * GROUP : (s + 1) * GROUP, h * VALUE : (h + 1) * VALUE] = out.astype(bf16)
+            here = slice(s * GROUP, (s + 1) * GROUP)
+            lanes = slice(h * VALUE, (h + 1) * VALUE)
+            low = out.astype(bf16)
+            mixed_ref[here, lanes] = low
+            low = low.astype(f32)
+            gate = gate_ref[here, lanes]
+            scale = lax.rsqrt(jnp.mean(low * low, axis=1, keepdims=True) + epsilon)
+            gated = low * scale * gain_ref[0:1] * (gate * sigmoid(gate))
+            gated_ref[here, lanes] = gated.astype(bf16)
             leaving = (block.leaving[:, h : h + 1] * block.keys[h]).astype(bf16)
             keep = block.retain[:, h : h + 1]
             own = slice(h * KEY, (h + 1) * KEY)
@@ -284,32 +297,50 @@
 
 
 def backward_kernel(
-    heads, starts_ref, raw_ref, filters_ref, decay_ref,
-    mixed_grad_ref, inverse_ref, delta_ref, rest_ref, memory_ref,
-    raw_grad_ref, filters_grad_ref, decay_grad_ref, state, halo,
+    heads, starts_ref, raw_ref, value_ref, filters_ref, decay_ref, gate_ref, gain_ref,
+    gated_grad_ref, mixed_ref, inverse_ref, delta_ref, rest_ref, memory_ref,
+    raw_grad_ref, value_grad_ref, gate_grad_ref, filters_grad_ref, decay_grad_ref, gain_grad_ref,
+    state, halo,
 ):
     step = pl.program_id(0)
     steps = pl.num_programs(0)
-    width = heads * (2 * KEY + VALUE)
+    width = 2 * heads * KEY
 
     @pl.when(step == 0)
     def _():
         state[...] = jnp.zeros_like(state)
+        gain_grad_ref[...] = jnp.zeros_like(gain_grad_ref)
         halo[...] = jnp.zeros_like(halo)
         filters_grad_ref[...] = jnp.zeros_like(filters_grad_ref)
         decay_grad_ref[...] = jnp.zeros_like(decay_grad_ref)
 
     for s in range(SUB - 1, -1, -1):
         base = pl.multiple_of(((steps - 1 - step) * SUB + s) * GROUP, GROUP)
-        block = Block(heads, base, raw_ref, filters_ref, decay_ref, starts_ref)
+        block = Block(heads, base, raw_ref, value_ref, filters_ref, decay_ref, starts_ref)
         here = slice(s * GROUP, (s + 1) * GROUP)
         stacked = slice(s * heads * GROUP, (s + 1) * heads * GROUP)
         solve = inverse_ref[here]
         delta = delta_ref[stacked]
         rest = rest_ref[stacked]
-        out_grad = jnp.concatenate(
-            [mixed_grad_ref[here, h * VALUE : (h + 1) * VALUE] for h in range(heads)], axis=0
-        )
+        mixed_grads = []
+        for h in range(heads):
+            lanes = slice(h * VALUE, (h + 1) * VALUE)
+            grad = gated_grad_ref[here, lanes].astype(f32)
+            mixed = mixed_ref[here, lanes].astype(f32)
+            gate = gate_ref[here, lanes]
+            scale = lax.rsqrt(jnp.mean(mixed * mixed, axis=1, keepdims=True) + epsilon)
+            unit = mixed * scale
+            open_gate = sigmoid(gate)
+            swish = gate * open_gate
+            along = grad * unit
+            product = (along * swish).reshape(GROUP // 8, 8, VALUE)
+            gain_grad_ref[...] = gain_grad_ref[...] + jnp.sum(product, axis=0)
+            gate_grad = along * gain_ref[0:1] * (open_gate * (1.0 + gate * (1.0 - open_gate)))
+            gate_grad_ref[here, lanes] = gate_grad.astype(bf16)
+            unit_grad = grad * swish * gain_ref[0:1]
+            inner = jnp.mean(unit_grad * unit, axis=1, keepdims=True)
+            mixed_grads.append((scale * (unit_grad - unit * inner)).astype(bf16))
+        out_grad = jnp.concatenate(mixed_grads, axis=0)
         later = [state[h * KEY : (h + 1) * KEY] for h in range(heads)]
         later_low = [m.astype(bf16) for m in later]
         leaving = [
@@ -394,14 +425,14 @@
                 along = jnp.sum(grad * conv, axis=1, keepdims=True)
                 conv_grad = (factor * scale) * (grad - conv * (scale * scale * along))
                 convolve_back(
-                    block, s, start, KEY, conv_grad * silu_slope(pre), starts_ref,
+                    block, s, start, start, KEY, conv_grad * silu_slope(pre), starts_ref,
                     raw_grad_ref, filters_grad_ref, halo,
                 )
             start = 2 * heads * KEY + h * VALUE
             pre = block.convolve(start, VALUE)
             convolve_back(
-                block, s, start, VALUE, rest_grad[h] * silu_slope(pre), starts_ref,
-                raw_grad_ref, filters_grad_ref, halo,
+                block, s, start, h * VALUE, VALUE, rest_grad[h] * silu_slope(pre), starts_ref,
+                value_grad_ref, filters_grad_ref, halo,
             )
         entering_grad = columns(entering_grad) * block.entering
         leaving_grad = columns(leaving_grad) * block.leaving
@@ -428,7 +459,7 @@
 
 
 def convolve_back(
-    block, s, start, width, pre_grad, starts_ref, raw_grad_ref, filters_grad_ref, halo
+    block, s, start, place, width, pre_grad, starts_ref, grad_ref, filters_grad_ref, halo
 ):
     lanes = slice(start, start + width)
     taps = block.taps(start, width)
@@ -448,14 +479,14 @@
         mask = (docs == doc_count(starts_ref, times - o)).astype(f32)
         moved = pltpu.roll(extended * mask, rows - o, 0)[:GROUP]
         total = total + moved * filters[CONV - 1 - o : CONV - o]
-    raw_grad_ref[s * GROUP : (s + 1) * GROUP, lanes] = total.astype(bf16)
+    grad_ref[s * GROUP : (s + 1) * GROUP, place : place + width] = total.astype(bf16)
     halo[:, lanes] = pre_grad[:8]
 
 
 SPACE = 56 * 2**20
 
 
-def mixer_forward(raw, filters, decays, starts, heads):
+def mixer_forward(raw, values, filters, decays, starts, gates, gain, heads):
     length, wide = raw.shape
     steps = length // (SUB * GROUP)
     rows = SUB * GROUP
@@ -466,13 +497,24 @@
         functools.partial(forward_kernel, heads),
         grid=(steps,),
         in_specs=[
-            pl.BlockSpec(memory_space=pltpu.SMEM), whole(raw), whole(filters), whole(decays),
+            pl.BlockSpec(memory_space=pltpu.SMEM),
+            whole(raw),
+            whole(values),
+            whole(filters),
+            whole(decays),
+            part(rows, heads * VALUE),
+            whole(gain),
         ],
         out_specs=[
-            part(rows, heads * VALUE), part(rows, heads * GROUP), part(rows * heads, VALUE),
-            part(rows * heads, VALUE), part(SUB * heads * KEY, VALUE),
+            part(rows, heads * VALUE),
+            part(rows, heads * VALUE),
+            part(rows, heads * GROUP),
+            part(rows * heads, VALUE),
+            part(rows * heads, VALUE),
+            part(SUB * heads * KEY, VALUE),
         ],
         out_shape=[
+            jax.ShapeDtypeStruct((length, heads * VALUE), bf16),
             jax.ShapeDtypeStruct((length, heads * VALUE), bf16),
             jax.ShapeDtypeStruct((length, heads * GROUP), bf16),
             jax.ShapeDtypeStruct((length * heads, VALUE), bf16),
@@ -481,41 +523,64 @@
         ],
         scratch_shapes=[pltpu.VMEM((heads * KEY, VALUE), f32)],
         compiler_params=pltpu.CompilerParams(vmem_limit_bytes=SPACE),
+        cost_estimate=pl.CostEstimate(
+            flops=length * heads * 11_000_000, bytes_accessed=2**24, transcendentals=0
+        ),
         name="mixer_forward",
-    )(starts, raw, filters, decays)
-
-
-def mixer_backward(raw, filters, decays, starts, mixed_grad, kept, heads):
+    )(starts, raw, values, filters, decays, gates, gain)
+
+
+def mixer_backward(raw, values, filters, decays, starts, gates, gain, gated_grad, kept, heads):
     length, wide = raw.shape
     steps = length // (SUB * GROUP)
     rows = SUB * GROUP
     whole = lambda a: pl.BlockSpec(a.shape, lambda i: (0, 0))
+    same = lambda r, c: pl.BlockSpec((r, c), lambda i: (0, 0))
     part = lambda r, c: pl.BlockSpec((r, c), lambda i: (steps - 1 - i, 0))
     return pl.pallas_call(
         functools.partial(backward_kernel, heads),
         grid=(steps,),
         in_specs=[
-            pl.BlockSpec(memory_space=pltpu.SMEM), whole(raw), whole(filters), whole(decays),
-            part(rows, heads * VALUE), part(rows, heads * GROUP), part(rows * heads, VALUE),
-            part(rows * heads, VALUE), part(SUB * heads * KEY, VALUE),
+            pl.BlockSpec(memory_space=pltpu.SMEM),
+            whole(raw),
+            whole(values),
+            whole(filters),
+            whole(decays),
+            part(rows, heads * VALUE),
+            whole(gain),
+            part(rows, heads * VALUE),
+            part(rows, heads * VALUE),
+            part(rows, heads * GROUP),
+            part(rows * heads, VALUE),
+            part(rows * heads, VALUE),
+            part(SUB * heads * KEY, VALUE),
         ],
         out_specs=[
             part(rows, wide),
-            pl.BlockSpec((8 * CONV, filters.shape[1]), lambda i: (0, 0)),
-            pl.BlockSpec((2, heads), lambda i: (0, 0)),
+            part(rows, heads * VALUE),
+            part(rows, heads * VALUE),
+            same(8 * CONV, filters.shape[1]),
+            same(2, heads),
+            same(8, VALUE),
         ],
         out_shape=[
             jax.ShapeDtypeStruct((length, wide), bf16),
+            jax.ShapeDtypeStruct((length, heads * VALUE), bf16),
+            jax.ShapeDtypeStruct((length, heads * VALUE), bf16),
             jax.ShapeDtypeStruct((8 * CONV, filters.shape[1]), f32),
             jax.ShapeDtypeStruct((2, heads), f32),
+            jax.ShapeDtypeStruct((8, VALUE), f32),
         ],
         scratch_shapes=[
             pltpu.VMEM((heads * KEY, VALUE), f32),
             pltpu.VMEM((8, filters.shape[1]), f32),
         ],
         compiler_params=pltpu.CompilerParams(vmem_limit_bytes=SPACE),
+        cost_estimate=pl.CostEstimate(
+            flops=length * heads * 14_000_000, bytes_accessed=2**24, transcendentals=0
+        ),
         name="mixer_backward",
-    )(starts, raw, filters, decays, mixed_grad, *kept)
+    )(starts, raw, values, filters, decays, gates, gain, gated_grad, *kept)
 
 
 def forward_dot(left_side, right_side):
@@ -532,10 +597,6 @@
 
 def rms_norm(values, gain):
     return values * lax.rsqrt(jnp.mean(values * values, axis=-1, keepdims=True) + epsilon) * gain
-
-
-def gated_norm(values, gates, gain):
-    return rms_norm(values, gain) * jax.nn.silu(gates)
 
 
 def swiglu(gate_rows, up_rows):
@@ -583,6 +644,19 @@
     return lax.psum(values.astype(bf16), "seq").astype(f32)
 
 
+def own_first(values):
+    if lax.axis_size("seq") == 2:
+        return jnp.concatenate([values, swap_seq(values)], axis=0)
+    return lax.all_gather(values, "seq", axis=0, tiled=True)
+
+
+def sum_own_first(values):
+    if lax.axis_size("seq") == 2:
+        half = values.shape[0] // 2
+        return values[:half] + swap_seq(values[half:].astype(bf16)).astype(f32)
+    return sum_scatter_seq(values, 0)
+
+
 def exchange_seq(values, split, join):
     if lax.axis_size("seq") == 2:
         other = own_part(values, split, 1 - lax.axis_index("seq"))
@@ -590,12 +664,95 @@
     return lax.all_to_all(values, "seq", split_axis=split, concat_axis=join, tiled=True)
 
 
-def gather_shard(values):
-    return lax.all_gather(values, "shard", axis=0, tiled=True)
-
-
-def scatter_shard(values):
-    return lax.psum_scatter(values, "shard", scatter_dimension=0, tiled=True)
+PLACES = 4
+
+
+def in_grid():
+    return lax.axis_size("shard") == 4 * PLACES and lax.axis_size("seq") == 2
+
+
+def position():
+    place = lax.axis_index("shard")
+    return place // 4, (place // 2) % 2, place % 2
+
+
+def flip(values, mask):
+    size = lax.axis_size("shard")
+    return lax.ppermute(values, "shard", [(i, i ^ mask) for i in range(size)])
+
+
+def from_place(values, step):
+    size = lax.axis_size("shard")
+    return lax.ppermute(values, "shard", [(i, (i - 4 * step) % size) for i in range(size)])
+
+
+def assemble_kernel(place_ref, *refs):
+    *parts, out_ref = refs
+    own = place_ref[1] * 2 + place_ref[2]
+    for k, part in enumerate(parts):
+        out_ref[0, jnp.bitwise_xor(own, k)] = part[0]
+
+
+def gather_shard(values, direct=False):
+    if not direct or not in_grid():
+        return lax.all_gather(values, "shard", axis=0, tiled=True)
+    rows, columns = values.shape
+    along = jnp.concatenate([values] + [from_place(values, r) for r in range(1, PLACES)], axis=0)
+    beside = flip(along, 2)
+    parts = [along, flip(along, 1), beside, flip(beside, 1)]
+    place = jnp.stack(position()).astype(jnp.int32)
+    block = pl.BlockSpec((1, rows, columns), lambda r, place: (r, 0, 0))
+    full = pl.pallas_call(
+        assemble_kernel,
+        grid_spec=pltpu.PrefetchScalarGridSpec(
+            num_scalar_prefetch=1,
+            grid=(PLACES,),
+            in_specs=[block] * 4,
+            out_specs=pl.BlockSpec(
+                (1, 4, rows, columns), lambda r, place: (lax.rem(place[0] + r, PLACES), 0, 0, 0)
+            ),
+        ),
+        out_shape=jax.ShapeDtypeStruct((PLACES, 4, rows, columns), values.dtype),
+        compiler_params=pltpu.CompilerParams(vmem_limit_bytes=SPACE),
+        cost_estimate=pl.CostEstimate(
+            flops=0, bytes_accessed=64 * PLACES * rows * columns, transcendentals=0
+        ),
+        name="assemble",
+    )(place, *[p.reshape(PLACES, rows, columns) for p in parts])
+    return full.reshape(4 * PLACES * rows, columns)
+
+
+def scatter_shard(values, direct=False):
+    if not direct or not in_grid():
+        low = values.astype(bf16)
+        return lax.psum_scatter(low, "shard", scatter_dimension=0, tiled=True).astype(f32)
+    z, y, core = position()
+    rows, columns = values.shape
+    rows = rows // (4 * PLACES)
+
+    def pick(array, index, axis):
+        return lax.dynamic_index_in_dim(array, index, axis, keepdims=False)
+
+    values = values.reshape(PLACES, 2, 2, rows, columns)
+    held = pick(values, core, 2).astype(f32)
+    held = (held + flip(pick(values, 1 - core, 2).astype(bf16), 1).astype(f32)).astype(bf16)
+    kept = pick(held, y, 1).astype(f32)
+    held = (kept + flip(pick(held, 1 - y, 1), 2).astype(f32)).astype(bf16)
+    total = pick(held, z, 0).astype(f32)
+    for r in range(1, PLACES):
+        sent = pick(held, (z - r) % PLACES, 0)
+        total = total + from_place(sent, r).astype(f32)
+    return total
+
+
+def sum_small(values, axes):
+    if not in_grid():
+        return lax.psum(values, axes)
+    for mask in (1, 2, 4, 8):
+        values = values + flip(values, mask)
+    if "seq" in axes:
+        values = values + swap_seq(values)
+    return values
 
 
 def on_device(
@@ -620,14 +777,15 @@
     heads = HEADS // lax.axis_size("seq")
     shards = lax.axis_size("shard")
     rows = query_weight.shape[0]
-    width = heads * (2 * KEY + VALUE)
-    wide = width + KEY
+    width = 2 * heads * KEY
     ff = ffn_gate_weight.shape[1]
 
     logit_weight = own_part(beta_decay_weight.reshape(rows, HEADS, 2), 1)
     gain_rows = out_norm_gain.shape[0]
-    extra = jnp.concatenate(
+    raw_piece = jnp.concatenate(
         [
+            own_part(query_weight, 1),
+            own_part(key_weight, 1),
             logit_weight[:, :, 0],
             logit_weight[:, :, 1],
             norm_gain[:, None],
@@ -637,28 +795,40 @@
         ],
         axis=1,
     )
-    mixer_piece = jnp.concatenate(
-        [
-            own_part(query_weight, 1),
-            own_part(key_weight, 1),
-            own_part(value_weight, 1),
-            extra,
-            own_part(gate_weight, 1),
-        ],
-        axis=1,
-    )
-    mixer_full = gather_shard(mixer_piece)
-    out_full = gather_shard(out_weight)
-    ffn_full = gather_shard(jnp.concatenate([ffn_gate_weight, ffn_up_weight], axis=1))
-    down_full = gather_shard(down_weight)
-    raw_full = mixer_full[:, :wide]
-    gate_full = mixer_full[:, wide:]
-    first_gain = mixer_full[:, width + 2 * heads].astype(f32)
-    second_gain = mixer_full[:, width + 2 * heads + 1].astype(f32)
+    units = ff // shards // lax.axis_size("seq")
+
+    def own_units(weight):
+        return own_part(weight.reshape(rows, shards, ff // shards), 2).reshape(rows, shards * units)
+
+    gate_piece = own_part(gate_weight, 1)
+    raw_wide = raw_piece.shape[1]
+    first_full = gather_shard(jnp.concatenate([raw_piece, own_part(value_weight, 1)], axis=1))
+    raw_full = first_full[:, :raw_wide]
+    value_full = first_full[:, raw_wide:]
+    gate_full = gather_shard(gate_piece, direct=True)
+    half = shards * units
+    model = out_weight.shape[1]
+    out_wide = out_weight.size // rows
+    rest_full = gather_shard(
+        jnp.concatenate(
+            [
+                own_units(ffn_gate_weight),
+                own_units(ffn_up_weight),
+                out_weight.reshape(rows, out_wide),
+                own_part(down_weight, 0).reshape(rows, units * model // rows),
+            ],
+            axis=1,
+        )
+    )
+    ffn_full = rest_full[:, : 2 * half]
+    out_full = rest_full[:, 2 * half : 2 * half + out_wide].reshape(shards * out_weight.shape[0], model)
+    down_full = rest_full[:, 2 * half + out_wide :].reshape(half, model)
+    first_gain = raw_full[:, width + 2 * heads].astype(f32)
+    second_gain = raw_full[:, width + 2 * heads + 1].astype(f32)
     third_gain = (
-        mixer_full[:, width + 2 * heads + 2]
+        raw_full[:, width + 2 * heads + 2]
         .reshape(shards, rows)[:, :gain_rows]
-        .reshape(shards * gain_rows)
+        .reshape(1, shards * gain_rows)
         .astype(f32)
     )
 
@@ -672,6 +842,7 @@
     )
     normed = (all_scaled * first_gain).astype(bf16)
     raw = forward_dot(normed, raw_full).astype(bf16)
+    values = forward_dot(normed, value_full).astype(bf16)
     gate_rows = forward_dot(normed, gate_full)
     filters = jnp.concatenate(
         [
@@ -682,62 +853,71 @@
         axis=1,
     )
     decays = decay_params.T
-    mixed, *kept = mixer_forward(raw, filters, decays, doc_starts, heads)
-    gated, gated_pull = jax.vjp(
-        gated_norm,
-        mixed.astype(f32).reshape(length, heads, VALUE),
-        gate_rows.reshape(length, heads, VALUE),
-        third_gain,
-    )
-    gated_low = exchange_seq(gated.astype(bf16).reshape(length, heads * VALUE), 0, 1)
+    gated, *kept = mixer_forward(
+        raw, values, filters, decays, doc_starts, gate_rows, third_gain, heads
+    )
+    gated_low = exchange_seq(gated, 0, 1)
     middle = inputs + forward_dot(gated_low, out_full)
     second_norm, second_pull = jax.vjp(rms_norm, middle, second_gain)
-    hidden = second_norm.astype(bf16)
+    hidden = own_first(second_norm.astype(bf16))
+    cotangent = out_cotangent[0]
+    all_cotangent = own_first(cotangent)
     both_ffn = forward_dot(hidden, ffn_full)
-    activated, swiglu_pull = jax.vjp(swiglu, both_ffn[:, :ff], both_ffn[:, ff:])
+    activated, swiglu_pull = jax.vjp(swiglu, both_ffn[:, :half], both_ffn[:, half:])
     activated_low = activated.astype(bf16)
-    block_out = (middle + forward_dot(activated_low, down_full)).astype(bf16)
-
-    cotangent = out_cotangent[0]
-    act_grad = times_transposed(cotangent, down_full)
-    down_grad = transposed_times(activated_low, cotangent).astype(bf16)
+    act_grad = times_transposed(all_cotangent, down_full)
     both_grad = jnp.concatenate([g.astype(bf16) for g in swiglu_pull(act_grad)], axis=1)
+    hidden_grad = sum_own_first(times_transposed(both_grad, ffn_full))
+    block_out = (middle + sum_own_first(forward_dot(activated_low, down_full))).astype(bf16)
+    down_grad = transposed_times(activated_low, all_cotangent).astype(bf16)
     ffn_grad = transposed_times(hidden, both_grad).astype(bf16)
-    hidden_grad = times_transposed(both_grad, ffn_full)
     middle_part, ffn_gain_grad = second_pull(hidden_grad)
     middle_grad = cotangent.astype(f32) + middle_part
     branch_low = middle_grad.astype(bf16)
     out_grad = transposed_times(gated_low, branch_low).astype(bf16)
     gated_grad = exchange_seq(times_transposed(branch_low, out_full).astype(bf16), 1, 0)
-    mixed_grad, gate_rows_grad, out_gain_grad = gated_pull(
-        gated_grad.astype(f32).reshape(length, heads, VALUE)
-    )
-    raw_grad, filters_grad, decays_grad = mixer_backward(
+    raw_grad, value_grad, gate_grad, filters_grad, decays_grad, out_gain_grad = mixer_backward(
         raw,
+        values,
         filters,
         decays,
         doc_starts,
-        mixed_grad.astype(bf16).reshape(length, heads * VALUE),
+        gate_rows,
+        third_gain,
+        gated_grad,
         kept,
         heads,
     )
-    gate_low = gate_rows_grad.astype(bf16).reshape(length, heads * VALUE)
-    normed_grad = times_transposed(raw_grad, raw_full) + times_transposed(gate_low, gate_full)
+    normed_grad = (
+        times_transposed(raw_grad, raw_full)
+        + times_transposed(value_grad, value_full)
+        + times_transposed(gate_grad, gate_full)
+    )
     raw_weight_grad = transposed_times(normed, raw_grad).astype(bf16)
-    gate_weight_grad = transposed_times(normed, gate_low).astype(bf16)
+    value_weight_grad = transposed_times(normed, value_grad).astype(bf16)
+    gate_weight_grad = transposed_times(normed, gate_grad).astype(bf16)
     norm_gain_grad = jnp.sum(normed_grad * all_scaled, axis=0)
     own_normed_grad = sum_scatter_seq(normed_grad, 0)
     _, first_pull = jax.vjp(lambda v: rms_norm(v, first_gain), inputs)
     tokens_grad = middle_grad + first_pull(own_normed_grad)[0]
 
-    down_share = sum_seq(scatter_shard(down_grad))
-    ffn_share = sum_seq(scatter_shard(ffn_grad))
-    out_share = sum_seq(scatter_shard(out_grad))
-    gate_share = gather_seq(scatter_shard(gate_weight_grad), 1).astype(f32)
-    raw_share = scatter_shard(raw_weight_grad)
+    down_share = gather_seq(scatter_shard(down_grad).astype(bf16), 0).astype(f32)
+    ffn_share = scatter_shard(ffn_grad).astype(bf16)
+
+    def all_units(share):
+        share = gather_seq(share.reshape(rows, shards, units), 2)
+        return share.reshape(rows, ff).astype(f32)
+
+    ffn_gate_share = all_units(ffn_share[:, :half])
+    ffn_up_share = all_units(ffn_share[:, half:])
+    out_share = sum_seq(scatter_shard(out_grad, direct=True))
+    value_share = scatter_shard(value_weight_grad, direct=True).astype(bf16)
+    value_share = gather_seq(value_share, 1).astype(f32)
+    gate_share = scatter_shard(gate_weight_grad, direct=True).astype(bf16)
+    gate_share = gather_seq(gate_share, 1).astype(f32)
+    raw_share = scatter_shard(raw_weight_grad, direct=True).astype(bf16)
     query_share = gather_seq(raw_share[:, : heads * KEY], 1).astype(f32)
-    key_share = gather_seq(raw_share[:, heads * KEY : 2 * heads * KEY], 1).astype(f32)
-    value_share = gather_seq(raw_share[:, 2 * heads * KEY : width], 1).astype(f32)
+    key_share = gather_seq(raw_share[:, heads * KEY : width], 1).astype(f32)
     logit_share = jnp.stack(
         [
             raw_share[:, width : width + heads],
@@ -747,8 +927,12 @@
     ).reshape(rows, 2 * heads)
     logit_share = gather_seq(logit_share, 1).astype(f32)
 
-    filters_grad = jnp.sum(filters_grad.reshape(CONV, 8, width), axis=1)
-    filters_grad, decays_grad = lax.psum((filters_grad, decays_grad), "shard")
+    all_width = filters.shape[1]
+    filters_grad = jnp.sum(filters_grad.reshape(CONV, 8, all_width), axis=1)
+    own_sum = jnp.concatenate([filters_grad.reshape(CONV * all_width), decays_grad.reshape(-1)])
+    own_sum = sum_small(own_sum, ("shard",))
+    filters_grad = own_sum[: CONV * all_width].reshape(CONV, all_width)
+    decays_grad = own_sum[CONV * all_width :].reshape(2, heads)
     split = (heads * KEY, 2 * heads * KEY)
     filters_out = jnp.concatenate(
         [
@@ -758,7 +942,16 @@
         ],
         axis=2,
     )
-    gains = lax.psum((norm_gain_grad, out_gain_grad, ffn_gain_grad), ("seq", "shard"))
+    lengths = [shards * n for n in (norm_gain.shape[0], gain_rows, ffn_norm_gain.shape[0])]
+    gains = sum_small(
+        jnp.concatenate([norm_gain_grad, jnp.sum(out_gain_grad, axis=0), ffn_gain_grad]),
+        ("seq", "shard"),
+    )
+    gains = [
+        gains[: lengths[0]],
+        gains[lengths[0] : lengths[0] + lengths[1]],
+        gains[lengths[0] + lengths[1] :],
+    ]
     place = lax.axis_index("shard")
     gains = [
         lax.dynamic_slice_in_dim(g, place * (g.shape[0] // shards), g.shape[0] // shards)
@@ -778,8 +971,8 @@
         gains[1],
         out_share,
         gains[2],
-        ffn_share[:, :ff],
-        ffn_share[:, ff:],
+        ffn_gate_share,
+        ffn_up_share,
         down_share,
     )
 

time: 829 us -> 606 us (0.73)
  waiting for transfers between devices: 381 us -> 207 us
  blocking collectives: 97.9 us -> 0 us
  starting transfers between devices: 17.5 us -> 60.3 us
  matrix products: 125 us -> 106 us
  Pallas kernels: 93.7 us -> 109 us
  local copies, waits for them, and re-layouts: 52.9 us -> 64.8 us
    reduce_scatter x5 -> x2, waiting for transfers between devices: 196 us -> 0.01 us  [scatter_shard(): lax.psum_scatter(low, 'shard', scatter_dimension=0, tiled=True).astype(f32)]
    psum x2 -> x0, blocking collectives: 97.9 us -> none  [the longest x1 59.2 us: on_device(): filters_grad, decays_grad = lax.psum((filters_grad, decays_grad), 'shard')]
    ppermute x0 -> x34, waiting for transfers between devices: none -> 73 us  [the longest x15 36.8 us: from_place(): lax.ppermute(values, 'shard', [(i, (i - 4 * step) % size) for i in range(...]
    all_gather x4 -> x2, waiting for transfers between devices: 108 us -> 50.9 us  [gather_shard(): return lax.all_gather(values, 'shard', axis=0, tiled=True)]
    ppermute x0 -> x34, starting transfers between devices: none -> 39.2 us  [the longest x15 27.6 us: from_place(): lax.ppermute(values, 'shard', [(i, (i - 4 * step) % size) for i in range(...]
    dot_general x10 -> x12, matrix products: 82.4 us -> 68.2 us  [dot(): lax.dot_general(a, b, (((ca,), (cb,)), ((), ())), preferred_element_type=...]
    slice x4 -> x12, local copies, waits for them, and re-layouts: 4.24 us -> 13.8 us  [the longest x1 4.74 us: on_device(): rest_full[:, 2 * half:2 * half + out_wide]]
    reshape x2 -> x12, local copies, waits for them, and re-layouts: 10.5 us -> 19.5 us  [the longest x1 7.12 us: on_device(): rest_full[:, 2 * half:2 * half + out_wide]]
  transfers between devices with their start and end apart: 21 -> 56, of which waited for: 11 -> 28; matrix products, arithmetic and copies ran while one was open for 19% -> 29% of each run, Pallas kernels for 11% -> 18%
where the time goes in v2:
time: 606 us; the launch traced here: 602 us
  waiting for transfers between devices  207 us (34%)
  Pallas kernels  109 us (18%)
  matrix products  106 us (17%)
  local copies, waits for them, and re-layouts  64.8 us (11%)
  starting transfers between devices  60.3 us (10%)
  other arithmetic  40.9 us (7%)
  between operations  15 us (2%)
    ppermute x18, waiting for transfers between devices, swap_seq(): return lax.ppermute(values, 'seq', [(0, 1), (1, 0)])  82.7 us
    dot_general x12, matrix products, dot(): lax.dot_general(a, b, (((ca,), (cb,)), ((), ())), preferred_element_type=...  68.2 us
    pallas_call x1, Pallas kernels, mixer_backward(): pl.pallas_call(functools.partial(backward_kernel, heads), grid=(steps,),...  59.2 us
    all_gather x2, waiting for transfers between devices, gather_shard(): return lax.all_gather(values, 'shard', axis=0, tiled=True)  50.9 us
    pallas_call x1, Pallas kernels, mixer_forward(): pl.pallas_call(functools.partial(forward_kernel, heads), grid=(steps,), i...  45 us
    dot_general x6, matrix products, forward_dot(): return jnp.dot(left_side, right_side, preferred_element_type=f32)  37.4 us
    ppermute x15, waiting for transfers between devices, from_place(): lax.ppermute(values, 'shard', [(i, (i - 4 * step) % size) for i in range(...  36.8 us
    ppermute x19, waiting for transfers between devices, flip(): return lax.ppermute(values, 'shard', [(i, i ^ mask) for i in range(size)])  36.2 us
  transfers between devices with their start and end apart: 56, of which 28 were waited for; matrix products, arithmetic and copies ran while one was open for 29% of the time, Pallas kernels for 18%

profile of v2, /device:TPU:0, one launch (start us, length us, event | category | flops | bytes accessed | tf_op | source)
XLA Modules:
  0.0 602.0 jit_solution(14158764420645464375)
XLA Ops:
  18.6 5.1 collective-permute-start.1
  26.4 4.0 collective-permute-done.1
  30.3 10.5 %collective-permute-done.2 = bf16[64,1024]{1,0:T(8,128)(2,1)S(1)} collective-permute-done((bf16[64,1024]{1,0:T(8,128)(2,1)S(1)}, bf16[64,1024]{1,0:T(8,128)(2,1)S(1)}, u32[]{:S(2)}, u32[]{:S(2)}) %collective-permute-start.2) | collective-permute-done | bytes 131104 | tf_op jit(solution)/shard_map/ppermute | solution.py:686
  42.6 11.1 %collective-permute-done.5 = bf16[256,1024]{1,0:T(8,128)(2,1)S(1)} collective-permute-done((bf16[256,1024]{1,0:T(8,128)(2,1)S(1)}, bf16[256,1024]{1,0:T(8,128)(2,1)S(1)}, u32[]{:S(2)}, u32[]{:S(2)}) %collective-permute-start.5) | collective-permute-done | bytes 524320 | tf_op jit(solution)/shard_map/ppermute | solution.py:681
  55.7 4.5 assemble.1
  60.3 17.6 %all-gather.3.cloned.1.call-done = bf16[1024,2176]{1,0:T(8,128)(2,1)} async-done(((bf16[64,2176]{1,0:T(8,128)(2,1)}), bf16[1024,2176]{1,0:T(8,128)(2,1)}) %all-gather.3.cloned.1.call-update) | async-done | bytes 4456464 | tf_op jit(solution)/shard_map/all_gather | solution.py:698
  81.4 7.5 %fusion.71.gate_ref = f32[1024,1024]{1,0:T(8,128)} fusion(bf16[1024,1024]{1,0:T(8,128)(2,1)} %bitcast.168, f32[1024]{0:T(1024)S(1)} %get-tuple-element.75, f32[1024]{0:T(1024)S(1)} %add_rsqrt_fusion, bf16[512,1024]{1,0:T(8,128)(2,1)S(1)} %bitcast.155, bf16[512,1024]{1,0:T(8,128)(2,1)S(1)} %collective-permute-done, pred[]{:T(512)S(6)} %eq.36), kind=kOutput, calls=%fused_computation.196 | convolution fusion | flops 2161115136 | bytes 8396801 | tf_op jit(solution)/shard_map/dot_general | solution.py:587
  88.9 5.5 convolution_convert_fusion.8.value_ref
  94.5 6.0 convolution_convert_fusion.3.raw_ref
  100.5 45.0 %mixer_forward.1 = (bf16[1024,1024]{1,0:T(8,128)(2,1)}, bf16[1024,1024]{1,0:T(8,128)(2,1)}, bf16[1024,256]{1,0:T(8,128)(2,1)}, bf16[4096,256]{1,0:T(8,128)(2,1)}...) custom-call(s32[1,4]{1,0:T(1,128)} %starts_ref.3, bf16[1024,1152]{1,0:T(8,128)(2,1)} %convolution_convert_fusion.3.raw_ref, ...), custom_call_target="tpu_custom_call" | custom-call | flops 45056000000 | bytes 16777216 | tf_op jit(solution)/shard_map/mixer_forward/pallas_call | solution.py:496
  145.5 2.7 constant_dynamic-slice_fusion.13
  149.6 33.3 %all-gather.5.cloned.1.call-done = bf16[1024,6272]{1,0:T(8,128)(2,1)} async-done(((bf16[64,6272]{1,0:T(8,128)(2,1)}), bf16[1024,6272]{1,0:T(8,128)(2,1)}) %all-gather.5.cloned.1.call-update) | async-done | bytes 12845072 | tf_op jit(solution)/shard_map/all_gather | solution.py:698
  182.9 4.7 slice.157
  187.6 7.1 %reshape.259 = bf16[2048,1024]{1,0:T(8,128)(2,1)} reshape(bf16[1024,2048]{1,0:T(8,128)(2,1)} %slice.157) | data formatting | bytes 8388608 | tf_op jit(solution)/shard_map/reshape | solution.py:824
  195.7 5.6 multiply_reduce_fusion.2
  204.6 3.6 slice.162
  208.2 6.8 %reshape.260 = bf16[1408,1024]{1,0:T(8,128)(2,1)} reshape(bf16[1024,1408]{1,0:T(8,128)(2,1)} %slice.162) | data formatting | bytes 5767168 | tf_op jit(solution)/shard_map/reshape | solution.py:825
  215.0 13.9 %collective-permute-done.8 = bf16[512,1024]{1,0:T(8,128)(2,1)} collective-permute-done((bf16[512,1024]{1,0:T(8,128)(2,1)}, bf16[512,1024]{1,0:T(8,128)(2,1)}, u32[]{:S(2)}, u32[]{:S(2)}) %collective-permute-start.8) | collective-permute-done | bytes 1048608 | tf_op jit(solution)/shard_map/ppermute | solution.py:607
  228.9 9.4 %fusion.6 = f32[1024,2816]{1,0:T(8,128)S(1)} fusion(bf16[1024,6272]{1,0:T(8,128)(2,1)} %all-gather.5.cloned.1.call-done, bf16[512,1024]{1,0:T(8,128)(2,1)} %collective-permute-done.8, bf16[512,1024]{1,0:T(8,128)(2,1)} %multiply_convert_fusion.2), kind=kOutput, calls=%fused_computation.14 | convolution fusion | flops 5909774336 | bytes 19398656 | tf_op jit(solution)/shard_map/dot_general | solution.py:587
  238.3 12.4 %collective-permute-done.10 = bf16[512,1024]{1,0:T(8,128)(2,1)} collective-permute-done((bf16[512,1024]{1,0:T(8,128)(2,1)}, bf16[512,1024]{1,0:T(8,128)(2,1)}, u32[]{:S(2)}, u32[]{:S(2)}) %collective-permute-start.10) | collective-permute-done | bytes 1048608 | tf_op jit(solution)/shard_map/ppermute | solution.py:607
  250.7 9.3 %fusion.2 = (bf16[1024,1408]{1,0:T(8,128)(2,1)}, bf16[1024,1408]{1,0:T(8,128)(2,1)}, bf16[1024,1408]{1,0:T(8,128)(2,1)}) fusion(f32[1024,2816]{1,0:T(8,128)S(1)} %fusion.6, bf16[1408,1024]{1,0:T(8,128)(2,1)S(1)} %copy-done.16, bf16[512,1024]{1,0:T(8,128)(2,1)} %collective-permute-done.10, bf16[512,1024]{1,0:T(8,128)(2,1)} %bitcast.17), kind=kOutput, calls=%fused_computation.3 | convolution fusion | flops 2980052992 | bytes 25165824 | tf_op jit(solution)/shard_map/dot_general | solution.py:23
  260.0 7.2 %convolution_convert_fusion.4 = bf16[1408,1024]{1,0:T(8,128)(2,1)} fusion(bf16[1024,1408]{1,0:T(8,128)(2,1)} %get-tuple-element.80, bf16[512,1024]{1,0:T(8,128)(2,1)} %collective-permute-done.10, bf16[512,1024]{1,0:T(8,128)(2,1)} %bitcast.17), kind=kOutput, calls=%fused_computation.27 | convolution fusion | flops 2958426112 | bytes 7864320 | tf_op jit(solution)/shard_map/dot_general | solution.py:23
  267.3 10.2 %fusion.4 = f32[1024,1024]{1,0:T(8,128)S(1)} fusion(bf16[1024,6272]{1,0:T(8,128)(2,1)} %all-gather.5.cloned.1.call-done, bf16[1024,1408]{1,0:T(8,128)(2,1)} %get-tuple-element.79, bf16[1024,1408]{1,0:T(8,128)(2,1)} %get-tuple-element.78), kind=kOutput, calls=%fused_computation.12 | convolution fusion | flops 5917114368 | bytes 15728640 | tf_op jit(solution)/shard_map/dot_general | solution.py:23
  280.3 3.4 fusion.79
  286.6 18.6 %collective-permute-done.11 = bf16[512,1024]{1,0:T(8,128)(2,1)} collective-permute-done((bf16[512,1024]{1,0:T(8,128)(2,1)}, bf16[512,1024]{1,0:T(8,128)(2,1)}, u32[]{:S(2)}, u32[]{:S(2)}) %collective-permute-start.11) | collective-permute-done | bytes 1048608 | tf_op jit(solution)/shard_map/ppermute | solution.py:607
  307.8 18.2 %collective-permute-done.9 = bf16[512,1024]{1,0:T(8,128)(2,1)} collective-permute-done((bf16[512,1024]{1,0:T(8,128)(2,1)}, bf16[512,1024]{1,0:T(8,128)(2,1)}, u32[]{:S(2)}, u32[]{:S(2)}) %collective-permute-start.9) | collective-permute-done | bytes 1048608 | tf_op jit(solution)/shard_map/ppermute | solution.py:607
  326.1 4.5 fusion.15
  336.0 10.4 %convolution_convert_fusion = bf16[1024,2816]{1,0:T(8,128)(2,1)} fusion(bf16[1024,1408]{1,0:T(8,128)(2,1)S(1)} %copy-done.41, bf16[1024,1408]{1,0:T(8,128)(2,1)S(1)} %copy-done.40, bf16[512,1024]{1,0:T(8,128)(2,1)} %collective-permute-done.8, bf16[512,1024]{1,0:T(8,128)(2,1)} %multiply_convert_fusion.2), kind=kOutput, calls=%fused_computation.9 | convolution fusion | flops 5924192256 | bytes 13631488 | tf_op jit(solution)/shard_map/dot_general | solution.py:23
  348.0 4.8 convolution_convert_fusion.1
  354.9 3.5 collective-permute-done.12
  358.4 4.0 maximum_select_fusion.2.gated_grad_ref
  362.5 59.2 %mixer_backward.1 = (bf16[1024,1152]{1,0:T(8,128)(2,1)}, bf16[1024,1024]{1,0:T(8,128)(2,1)}, bf16[1024,1024]{1,0:T(8,128)(2,1)}, f32[32,2048]{1,0:T(8,128)}, f32[2,4]{1,0:T(2,128)}, /*index=5*/f32[8,256]{1,0:T(8,128)}) custom-call(s32[1,4]{1,0:T(1,128)} %starts_ref.3, bf16[1024,1152]{1,0:T(8,128)(2,1)} %convolution_convert_fusion.3.raw_ref, ...), custom_call_target="tpu_custom_call" | custom-call | flops 57344000000 | bytes 16777216 | tf_op jit(solution)/shard_map/mixer_backward/pallas_call | solution.py:540
  423.5 5.6 convolution_convert_fusion.2
  432.2 5.4 fusion.25
  437.7 4.2 fusion.28
  441.9 2.9 fusion.11
  444.9 3.0 convolution_convert_fusion.6
  451.8 2.8 convolution_convert_fusion.7
  483.0 12.2 %collective-permute-done.13 = bf16[512,1024]{1,0:T(8,128)(2,1)} collective-permute-done((bf16[512,1024]{1,0:T(8,128)(2,1)}, bf16[512,1024]{1,0:T(8,128)(2,1)}, u32[]{:S(2)}, u32[]{:S(2)}) %collective-permute-start.13) | collective-permute-done | bytes 1048608 | tf_op jit(solution)/shard_map/ppermute | solution.py:607
  497.1 3.3 fusion.17
  502.8 10.9 %collective-permute-done.33 = bf16[4,64,1024]{2,1,0:T(8,128)(2,1)S(1)} collective-permute-done((bf16[4,64,1024]{2,1,0:T(8,128)(2,1)S(1)}, bf16[4,64,1024]{2,1,0:T(8,128)(2,1)S(1)}, u32[]{:S(2)}, u32[]{:S(2)}) %collective-permute-start.33) | collective-permute-done | bytes 524320 | tf_op jit(solution)/shard_map/ppermute | solution.py:681
  516.8 8.3 %collective-permute-done.27 = bf16[4,64,1024]{2,1,0:T(8,128)(2,1)S(1)} collective-permute-done((bf16[4,64,1024]{2,1,0:T(8,128)(2,1)S(1)}, bf16[4,64,1024]{2,1,0:T(8,128)(2,1)S(1)}, u32[]{:S(2)}, u32[]{:S(2)}) %collective-permute-start.27) | collective-permute-done | bytes 524320 | tf_op jit(solution)/shard_map/ppermute | solution.py:681
  529.2 3.5 collective-permute-done.36
  541.2 3.6 collective-permute-start.21
  547.9 5.7 collective-permute-done.22
  559.6 6.9 %collective-permute-start.46 = (bf16[128,1024]{1,0:T(8,128)(2,1)S(1)}, bf16[128,1024]{1,0:T(8,128)(2,1)S(1)}, u32[]{:S(2)}, u32[]{:S(2)}) collective-permute-start(bf16[128,1024]{1,0:T(8,128)(2,1)S(1)} %get-tuple-element.95), channel_id=1, source_target_pairs={{0,8},{1,9},{2,10},{3,11},{4,12},{5,13},{6,14},{7,15},{8,0},{9,1},... | collective-permute-start | bytes 786440 | tf_op jit(solution)/shard_map/ppermute | solution.py:686
  571.9 7.3 %collective-permute-done.46 = bf16[128,1024]{1,0:T(8,128)(2,1)S(1)} collective-permute-done((bf16[128,1024]{1,0:T(8,128)(2,1)S(1)}, bf16[128,1024]{1,0:T(8,128)(2,1)S(1)}, u32[]{:S(2)}, u32[]{:S(2)}) %collective-permute-start.46) | collective-permute-done | bytes 262176 | tf_op jit(solution)/shard_map/ppermute | solution.py:686
  587.6 2.9 collective-permute-done.50
  (308 shorter events, 128.8 us)
Async XLA Ops:
  7.2 70.7 %all-gather.3.cloned.1.call-start = ((), (), s32[]{:S(2)}) async-start(), calls=%async_computation.2 | async-start | bytes 4734976 | tf_op jit(solution)/shard_map/all_gather | solution.py:698
  13.3 169.6 %all-gather.5.cloned.1.call-start = ((), (), s32[]{:S(2)}) async-start(), calls=%async_computation.3 | async-start | bytes 13647872 | tf_op jit(solution)/shard_map/all_gather | solution.py:698
  18.5 552.3 %reduce-scatter.5.cloned.1.call-start = ((), (), s32[]{:S(2)}) async-start(), calls=%async_computation.5 | async-start | bytes 3063808 | tf_op jit(solution)/shard_map/reduce_scatter | solution.py:728
  18.6 11.8 %collective-permute-start.1 = (bf16[64,1024]{1,0:T(8,128)(2,1)S(1)}, bf16[64,1024]{1,0:T(8,128)(2,1)S(1)}, u32[]{:S(2)}, u32[]{:S(2)}) collective-permute-start(bf16[64,1024]{1,0:T(8,128)(2,1)S(1)} %constant_dynamic-slice_fusion.14), channel_id=1, source_target_pairs={{0,12},{1,13},{2,14},{3,15},{4,0},{5,1},{6,2},{7,3},{8,4},{9,5},{1... | collective-permute-start | bytes 393224 | tf_op jit(solution)/shard_map/ppermute | solution.py:686
  23.7 17.2 %collective-permute-start.2 = (bf16[64,1024]{1,0:T(8,128)(2,1)S(1)}, bf16[64,1024]{1,0:T(8,128)(2,1)S(1)}, u32[]{:S(2)}, u32[]{:S(2)}) collective-permute-start(bf16[64,1024]{1,0:T(8,128)(2,1)S(1)} %constant_dynamic-slice_fusion.14), channel_id=1, source_target_pairs={{0,8},{1,9},{2,10},{3,11},{4,12},{5,13},{6,14},{7,15},{8,0},{9,1},... | collective-permute-start | bytes 393224 | tf_op jit(solution)/shard_map/ppermute | solution.py:686
  23.7 17.2 %collective-permute-start.3 = (bf16[64,1024]{1,0:T(8,128)(2,1)S(1)}, bf16[64,1024]{1,0:T(8,128)(2,1)S(1)}, u32[]{:S(2)}, u32[]{:S(2)}) collective-permute-start(bf16[64,1024]{1,0:T(8,128)(2,1)S(1)} %constant_dynamic-slice_fusion.14), channel_id=1, source_target_pairs={{0,4},{1,5},{2,6},{3,7},{4,8},{5,9},{6,10},{7,11},{8,12},{9,13},{1... | collective-permute-start | bytes 393224 | tf_op jit(solution)/shard_map/ppermute | solution.py:686
  24.8 29.5 %collective-permute-start = (bf16[512,1024]{1,0:T(8,128)(2,1)S(1)}, bf16[512,1024]{1,0:T(8,128)(2,1)S(1)}, u32[]{:S(2)}, u32[]{:S(2)}) collective-permute-start(bf16[512,1024]{1,0:T(8,128)(2,1)S(1)} %bitcast.153), channel_id=1, source_target_pairs={{0,16},{16,0},{1,17},{17,1},{2,18},{18,2},{3,19},{19,3},{4,20},{20... | collective-permute-start | bytes 3145736 | tf_op jit(solution)/shard_map/ppermute | solution.py:607
  40.9 12.8 %collective-permute-start.5 = (bf16[256,1024]{1,0:T(8,128)(2,1)S(1)}, bf16[256,1024]{1,0:T(8,128)(2,1)S(1)}, u32[]{:S(2)}, u32[]{:S(2)}) collective-permute-start(bf16[256,1024]{1,0:T(8,128)(2,1)S(1)} %pad_maximum_fusion.10), channel_id=1, source_target_pairs={{0,2},{1,3},{2,0},{3,1},{4,6},{5,7},{6,4},{7,5},{8,10},{9,11},{10,... | collective-permute-start | bytes 1572872 | tf_op jit(solution)/shard_map/ppermute | solution.py:681
  42.5 12.6 %collective-permute-start.4 = (bf16[256,1024]{1,0:T(8,128)(2,1)S(1)}, bf16[256,1024]{1,0:T(8,128)(2,1)}, u32[]{:S(2)}, u32[]{:S(2)}) collective-permute-start(bf16[256,1024]{1,0:T(8,128)(2,1)S(1)} %pad_maximum_fusion.10), channel_id=1, source_target_pairs={{0,1},{1,0},{2,3},{3,2},{4,5},{5,4},{6,7},{7,6},{8,9},{9,8},{10,11... | collective-permute-start | bytes 1572872 | tf_op jit(solution)/shard_map/ppermute | solution.py:681
  148.2 46.6 %collective-permute-start.7 = (bf16[512,1024]{1,0:T(8,128)(2,1)S(1)}, bf16[512,1024]{1,0:T(8,128)(2,1)S(1)}, u32[]{:S(2)}, u32[]{:S(2)}) collective-permute-start(bf16[512,1024]{1,0:T(8,128)(2,1)S(1)} %get-tuple-element.92), channel_id=1, source_target_pairs={{0,16},{16,0},{1,17},{17,1},{2,18},{18,2},{3,19},{19,3},{4,20},{20... | collective-permute-start | bytes 3145736 | tf_op jit(solution)/shard_map/ppermute | solution.py:607
  202.6 26.3 %collective-permute-start.8 = (bf16[512,1024]{1,0:T(8,128)(2,1)}, bf16[512,1024]{1,0:T(8,128)(2,1)}, u32[]{:S(2)}, u32[]{:S(2)}) collective-permute-start(bf16[512,1024]{1,0:T(8,128)(2,1)} %multiply_convert_fusion.2), channel_id=1, source_target_pairs={{0,16},{16,0},{1,17},{17,1},{2,18},{18,2},{3,19},{19,3},{4,20},{20... | collective-permute-start | bytes 3145736 | tf_op jit(solution)/shard_map/ppermute | solution.py:607
  204.1 46.6 %collective-permute-start.10 = (bf16[512,1024]{1,0:T(8,128)(2,1)}, bf16[512,1024]{1,0:T(8,128)(2,1)}, u32[]{:S(2)}, u32[]{:S(2)}) collective-permute-start(bf16[512,1024]{1,0:T(8,128)(2,1)} %bitcast.17), channel_id=1, source_target_pairs={{0,16},{16,0},{1,17},{17,1},{2,18},{18,2},{3,19},{19,3},{4,20},{20... | collective-permute-start | bytes 3145736 | tf_op jit(solution)/shard_map/ppermute | solution.py:607
  267.2 315.3 %reduce-scatter.3.cloned.1.call-start = ((), (), s32[]{:S(2)}) async-start(), calls=%async_computation.4 | async-start | bytes 6127616 | tf_op jit(solution)/shard_map/reduce_scatter | solution.py:728
  278.8 26.4 %collective-permute-start.11 = (bf16[512,1024]{1,0:T(8,128)(2,1)}, bf16[512,1024]{1,0:T(8,128)(2,1)}, u32[]{:S(2)}, u32[]{:S(2)}) collective-permute-start(bf16[512,1024]{1,0:T(8,128)(2,1)} %slice.226), channel_id=1, source_target_pairs={{0,16},{16,0},{1,17},{17,1},{2,18},{18,2},{3,19},{19,3},{4,20},{20... | collective-permute-start | bytes 3145736 | tf_op jit(solution)/shard_map/ppermute | solution.py:607
  286.1 40.0 %collective-permute-start.9 = (bf16[512,1024]{1,0:T(8,128)(2,1)}, bf16[512,1024]{1,0:T(8,128)(2,1)}, u32[]{:S(2)}, u32[]{:S(2)}) collective-permute-start(bf16[512,1024]{1,0:T(8,128)(2,1)} %slice.227), channel_id=1, source_target_pairs={{0,16},{16,0},{1,17},{17,1},{2,18},{18,2},{3,19},{19,3},{4,20},{20... | collective-permute-start | bytes 3145736 | tf_op jit(solution)/shard_map/ppermute | solution.py:607
  334.5 23.9 %collective-permute-start.12 = (bf16[512,1024]{1,0:T(8,128)(2,1)}, bf16[512,1024]{1,0:T(8,128)(2,1)}, u32[]{:S(2)}, u32[]{:S(2)}) collective-permute-start(bf16[512,1024]{1,0:T(8,128)(2,1)} %get-tuple-element.88), channel_id=1, source_target_pairs={{0,16},{16,0},{1,17},{17,1},{2,18},{18,2},{3,19},{19,3},{4,20},{20... | collective-permute-start | bytes 3145736 | tf_op jit(solution)/shard_map/ppermute | solution.py:607
  354.9 117.7 %collective-permute-start.43 = (bf16[4,2,128,1024]{3,2,0,1:T(8,128)(2,1)}, bf16[4,2,128,1024]{3,2,0,1:T(8,128)(2,1)}, u32[]{:S(2)}, u32[]{:S(2)}) collective-permute-start(bf16[4,2,128,1024]{3,2,0,1:T(8,128)(2,1)} %bitcast.150), channel_id=1, source_target_pairs={{0,1},{1,0},{2,3},{3,2},{4,5},{5,4},{6,7},{7,6},{8,9},{9,8},{10,11... | collective-permute-start | bytes 6291464 | tf_op jit(solution)/shard_map/ppermute | solution.py:681
  423.5 33.5 %collective-permute-start.39 = (f32[8200]{0:T(1024)S(1)}, f32[8200]{0:T(1024)S(1)}, u32[]{:S(2)}, u32[]{:S(2)}) collective-permute-start(f32[8200]{0:T(1024)S(1)} %constant_dynamic-update-slice_fusion.4), channel_id=1, source_target_pairs={{0,1},{1,0},{2,3},{3,2},{4,5},{5,4},{6,7},{7,6},{8,9},{9,8},{10,11... | collective-permute-start | bytes 98408 | tf_op jit(solution)/shard_map/ppermute | solution.py:681
  431.7 68.7 %collective-permute-start.19 = (bf16[4,2,64,1152]{3,2,1,0:T(8,128)(2,1)}, bf16[4,2,64,1152]{3,2,1,0:T(8,128)(2,1)}, u32[]{:S(2)}, u32[]{:S(2)}) collective-permute-start(bf16[4,2,64,1152]{3,2,1,0:T(8,128)(2,1)} %dynamic-slice_bitcast_fusion), channel_id=1, source_target_pairs={{0,1},{1,0},{2,3},{3,2},{4,5},{5,4},{6,7},{7,6},{8,9},{9,8},{10,11... | collective-permute-start | bytes 3538952 | tf_op jit(solution)/shard_map/ppermute | solution.py:681
  450.6 26.3 %collective-permute-start.32 = (bf16[4,2,64,1024]{3,2,0,1:T(8,128)(2,1)}, bf16[4,2,64,1024]{3,2,0,1:T(8,128)(2,1)}, u32[]{:S(2)}, u32[]{:S(2)}) collective-permute-start(bf16[4,2,64,1024]{3,2,0,1:T(8,128)(2,1)} %bitcast.151), channel_id=1, source_target_pairs={{0,1},{1,0},{2,3},{3,2},{4,5},{5,4},{6,7},{7,6},{8,9},{9,8},{10,11... | collective-permute-start | bytes 3145736 | tf_op jit(solution)/shard_map/ppermute | solution.py:681
  460.0 5.1 collective-permute-start.18
  465.1 14.9 %collective-permute-start.26 = (bf16[4,2,64,1024]{3,2,0,1:T(8,128)(2,1)}, bf16[4,2,64,1024]{3,2,0,1:T(8,128)(2,1)}, u32[]{:S(2)}, u32[]{:S(2)}) collective-permute-start(bf16[4,2,64,1024]{3,2,0,1:T(8,128)(2,1)} %bitcast.152), channel_id=1, source_target_pairs={{0,1},{1,0},{2,3},{3,2},{4,5},{5,4},{6,7},{7,6},{8,9},{9,8},{10,11... | collective-permute-start | bytes 3145736 | tf_op jit(solution)/shard_map/ppermute | solution.py:681
  470.5 24.7 %collective-permute-start.13 = (bf16[512,1024]{1,0:T(8,128)(2,1)}, bf16[512,1024]{1,0:T(8,128)(2,1)}, u32[]{:S(2)}, u32[]{:S(2)}) collective-permute-start(bf16[512,1024]{1,0:T(8,128)(2,1)} %dynamic-slice_convert_fusion), channel_id=1, source_target_pairs={{0,16},{16,0},{1,17},{17,1},{2,18},{18,2},{3,19},{19,3},{4,20},{20... | collective-permute-start | bytes 3145736 | tf_op jit(solution)/shard_map/ppermute | solution.py:607
  476.2 80.6 %collective-permute-start.44 = (bf16[4,128,1024]{2,1,0:T(8,128)(2,1)}, bf16[4,128,1024]{2,1,0:T(8,128)(2,1)}, u32[]{:S(2)}, u32[]{:S(2)}) collective-permute-start(bf16[4,128,1024]{2,1,0:T(8,128)(2,1)} %dynamic-slice_bitcast_fusion.1), channel_id=1, source_target_pairs={{0,2},{1,3},{2,0},{3,1},{4,6},{5,7},{6,4},{7,5},{8,10},{9,11},{10,... | collective-permute-start | bytes 3145736 | tf_op jit(solution)/shard_map/ppermute | solution.py:681
  478.9 34.9 %collective-permute-start.33 = (bf16[4,64,1024]{2,1,0:T(8,128)(2,1)S(1)}, bf16[4,64,1024]{2,1,0:T(8,128)(2,1)S(1)}, u32[]{:S(2)}, u32[]{:S(2)}) collective-permute-start(bf16[4,64,1024]{2,1,0:T(8,128)(2,1)S(1)} %dynamic-slice_bitcast_fusion.3), channel_id=1, source_target_pairs={{0,2},{1,3},{2,0},{3,1},{4,6},{5,7},{6,4},{7,5},{8,10},{9,11},{10,... | collective-permute-start | bytes 1572872 | tf_op jit(solution)/shard_map/ppermute | solution.py:681
  481.8 43.2 %collective-permute-start.27 = (bf16[4,64,1024]{2,1,0:T(8,128)(2,1)S(1)}, bf16[4,64,1024]{2,1,0:T(8,128)(2,1)S(1)}, u32[]{:S(2)}, u32[]{:S(2)}) collective-permute-start(bf16[4,64,1024]{2,1,0:T(8,128)(2,1)S(1)} %dynamic-slice_bitcast_fusion.4), channel_id=1, source_target_pairs={{0,2},{1,3},{2,0},{3,1},{4,6},{5,7},{6,4},{7,5},{8,10},{9,11},{10,... | collective-permute-start | bytes 1572872 | tf_op jit(solution)/shard_map/ppermute | solution.py:681
  502.0 38.9 %collective-permute-start.20 = (bf16[4,64,1152]{2,1,0:T(8,128)(2,1)S(1)}, bf16[4,64,1152]{2,1,0:T(8,128)(2,1)S(1)}, u32[]{:S(2)}, u32[]{:S(2)}) collective-permute-start(bf16[4,64,1152]{2,1,0:T(8,128)(2,1)S(1)} %dynamic-slice_bitcast_fusion.2), channel_id=1, source_target_pairs={{0,2},{1,3},{2,0},{3,1},{4,6},{5,7},{6,4},{7,5},{8,10},{9,11},{10,... | collective-permute-start | bytes 1769480 | tf_op jit(solution)/shard_map/ppermute | solution.py:681
  514.0 12.4 %collective-permute-start.34 = (bf16[64,1024]{1,0:T(8,128)(2,1)S(1)}, bf16[64,1024]{1,0:T(8,128)(2,1)S(1)}, u32[]{:S(2)}, u32[]{:S(2)}) collective-permute-start(bf16[64,1024]{1,0:T(8,128)(2,1)S(1)} %get-tuple-element.99), channel_id=1, source_target_pairs={{0,12},{1,13},{2,14},{3,15},{4,0},{5,1},{6,2},{7,3},{8,4},{9,5},{1... | collective-permute-start | bytes 393224 | tf_op jit(solution)/shard_map/ppermute | solution.py:686
  516.7 12.5 %collective-permute-start.35 = (bf16[64,1024]{1,0:T(8,128)(2,1)S(1)}, bf16[64,1024]{1,0:T(8,128)(2,1)S(1)}, u32[]{:S(2)}, u32[]{:S(2)}) collective-permute-start(bf16[64,1024]{1,0:T(8,128)(2,1)S(1)} %get-tuple-element.101), channel_id=1, source_target_pairs={{0,8},{1,9},{2,10},{3,11},{4,12},{5,13},{6,14},{7,15},{8,0},{9,1},... | collective-permute-start | bytes 393224 | tf_op jit(solution)/shard_map/ppermute | solution.py:686
  525.0 7.6 %collective-permute-start.36 = (bf16[64,1024]{1,0:T(8,128)(2,1)S(1)}, bf16[64,1024]{1,0:T(8,128)(2,1)S(1)}, u32[]{:S(2)}, u32[]{:S(2)}) collective-permute-start(bf16[64,1024]{1,0:T(8,128)(2,1)S(1)} %get-tuple-element.100), channel_id=1, source_target_pairs={{0,4},{1,5},{2,6},{3,7},{4,8},{5,9},{6,10},{7,11},{8,12},{9,13},{1... | collective-permute-start | bytes 393224 | tf_op jit(solution)/shard_map/ppermute | solution.py:686
  526.5 8.7 %collective-permute-start.28 = (bf16[64,1024]{1,0:T(8,128)(2,1)S(1)}, bf16[64,1024]{1,0:T(8,128)(2,1)S(1)}, u32[]{:S(2)}, u32[]{:S(2)}) collective-permute-start(bf16[64,1024]{1,0:T(8,128)(2,1)S(1)} %get-tuple-element.102), channel_id=1, source_target_pairs={{0,12},{1,13},{2,14},{3,15},{4,0},{5,1},{6,2},{7,3},{8,4},{9,5},{1... | collective-permute-start | bytes 393224 | tf_op jit(solution)/shard_map/ppermute | solution.py:686
  529.2 8.8 %collective-permute-start.29 = (bf16[64,1024]{1,0:T(8,128)(2,1)S(1)}, bf16[64,1024]{1,0:T(8,128)(2,1)S(1)}, u32[]{:S(2)}, u32[]{:S(2)}) collective-permute-start(bf16[64,1024]{1,0:T(8,128)(2,1)S(1)} %get-tuple-element.104), channel_id=1, source_target_pairs={{0,8},{1,9},{2,10},{3,11},{4,12},{5,13},{6,14},{7,15},{8,0},{9,1},... | collective-permute-start | bytes 393224 | tf_op jit(solution)/shard_map/ppermute | solution.py:686
  532.6 6.9 %collective-permute-start.30 = (bf16[64,1024]{1,0:T(8,128)(2,1)S(1)}, bf16[64,1024]{1,0:T(8,128)(2,1)S(1)}, u32[]{:S(2)}, u32[]{:S(2)}) collective-permute-start(bf16[64,1024]{1,0:T(8,128)(2,1)S(1)} %get-tuple-element.103), channel_id=1, source_target_pairs={{0,4},{1,5},{2,6},{3,7},{4,8},{5,9},{6,10},{7,11},{8,12},{9,13},{1... | collective-permute-start | bytes 393224 | tf_op jit(solution)/shard_map/ppermute | solution.py:686
  535.1 9.6 %collective-permute-start.37 = (bf16[64,1024]{1,0:T(8,128)(2,1)S(1)}, bf16[64,1024]{1,0:T(8,128)(2,1)S(1)}, u32[]{:S(2)}, u32[]{:S(2)}) collective-permute-start(bf16[64,1024]{1,0:T(8,128)(2,1)S(1)} %fusion.51), channel_id=1, source_target_pairs={{0,16},{16,0},{1,17},{17,1},{2,18},{18,2},{3,19},{19,3},{4,20},{20... | collective-permute-start | bytes 393224 | tf_op jit(solution)/shard_map/ppermute | solution.py:607
  539.6 7.0 %collective-permute-start.31 = (bf16[64,1024]{1,0:T(8,128)(2,1)S(1)}, bf16[64,1024]{1,0:T(8,128)(2,1)S(1)}, u32[]{:S(2)}, u32[]{:S(2)}) collective-permute-start(bf16[64,1024]{1,0:T(8,128)(2,1)S(1)} %fusion.54), channel_id=1, source_target_pairs={{0,16},{16,0},{1,17},{17,1},{2,18},{18,2},{3,19},{19,3},{4,20},{20... | collective-permute-start | bytes 393224 | tf_op jit(solution)/shard_map/ppermute | solution.py:607
  541.2 6.7 %collective-permute-start.21 = (bf16[64,1152]{1,0:T(8,128)(2,1)S(1)}, bf16[64,1152]{1,0:T(8,128)(2,1)S(1)}, u32[]{:S(2)}, u32[]{:S(2)}) collective-permute-start(bf16[64,1152]{1,0:T(8,128)(2,1)S(1)} %get-tuple-element.96), channel_id=1, source_target_pairs={{0,12},{1,13},{2,14},{3,15},{4,0},{5,1},{6,2},{7,3},{8,4},{9,5},{1... | collective-permute-start | bytes 442376 | tf_op jit(solution)/shard_map/ppermute | solution.py:686
  544.8 8.8 %collective-permute-start.22 = (bf16[64,1152]{1,0:T(8,128)(2,1)S(1)}, bf16[64,1152]{1,0:T(8,128)(2,1)S(1)}, u32[]{:S(2)}, u32[]{:S(2)}) collective-permute-start(bf16[64,1152]{1,0:T(8,128)(2,1)S(1)} %get-tuple-element.98), channel_id=1, source_target_pairs={{0,8},{1,9},{2,10},{3,11},{4,12},{5,13},{6,14},{7,15},{8,0},{9,1},... | collective-permute-start | bytes 442376 | tf_op jit(solution)/shard_map/ppermute | solution.py:686
  544.8 8.8 %collective-permute-start.23 = (bf16[64,1152]{1,0:T(8,128)(2,1)S(1)}, bf16[64,1152]{1,0:T(8,128)(2,1)S(1)}, u32[]{:S(2)}, u32[]{:S(2)}) collective-permute-start(bf16[64,1152]{1,0:T(8,128)(2,1)S(1)} %get-tuple-element.97), channel_id=1, source_target_pairs={{0,4},{1,5},{2,6},{3,7},{4,8},{5,9},{6,10},{7,11},{8,12},{9,13},{1... | collective-permute-start | bytes 442376 | tf_op jit(solution)/shard_map/ppermute | solution.py:686
  553.8 12.7 %collective-permute-start.38 = (bf16[64,8]{0,1:T(8,128)(2,1)S(1)}, bf16[64,8]{0,1:T(8,128)(2,1)S(1)}, u32[]{:S(2)}, u32[]{:S(2)}) collective-permute-start(bf16[64,8]{0,1:T(8,128)(2,1)S(1)} %bitcast.178), channel_id=1, source_target_pairs={{0,16},{16,0},{1,17},{17,1},{2,18},{18,2},{3,19},{19,3},{4,20},{20... | collective-permute-start | bytes 3080 | tf_op jit(solution)/shard_map/ppermute | solution.py:607
  554.8 14.6 %collective-permute-start.25 = (bf16[64,512]{1,0:T(8,128)(2,1)S(1)}, bf16[64,512]{1,0:T(8,128)(2,1)S(1)}, u32[]{:S(2)}, u32[]{:S(2)}) collective-permute-start(bf16[64,512]{1,0:T(8,128)(2,1)S(1)} %get-tuple-element.109), channel_id=1, source_target_pairs={{0,16},{16,0},{1,17},{17,1},{2,18},{18,2},{3,19},{19,3},{4,20},{20... | collective-permute-start | bytes 196616 | tf_op jit(solution)/shard_map/ppermute | solution.py:607
  555.9 14.1 %collective-permute-start.24 = (bf16[64,512]{1,0:T(8,128)(2,1)S(1)}, bf16[64,512]{1,0:T(8,128)(2,1)S(1)}, u32[]{:S(2)}, u32[]{:S(2)}) collective-permute-start(bf16[64,512]{1,0:T(8,128)(2,1)S(1)} %get-tuple-element.110), channel_id=1, source_target_pairs={{0,16},{16,0},{1,17},{17,1},{2,18},{18,2},{3,19},{19,3},{4,20},{20... | collective-permute-start | bytes 196616 | tf_op jit(solution)/shard_map/ppermute | solution.py:607
  558.6 13.3 %collective-permute-start.45 = (bf16[128,1024]{1,0:T(8,128)(2,1)S(1)}, bf16[128,1024]{1,0:T(8,128)(2,1)S(1)}, u32[]{:S(2)}, u32[]{:S(2)}) collective-permute-start(bf16[128,1024]{1,0:T(8,128)(2,1)S(1)} %get-tuple-element.93), channel_id=1, source_target_pairs={{0,12},{1,13},{2,14},{3,15},{4,0},{5,1},{6,2},{7,3},{8,4},{9,5},{1... | collective-permute-start | bytes 786440 | tf_op jit(solution)/shard_map/ppermute | solution.py:686
  559.6 19.6 %collective-permute-start.46 = (bf16[128,1024]{1,0:T(8,128)(2,1)S(1)}, bf16[128,1024]{1,0:T(8,128)(2,1)S(1)}, u32[]{:S(2)}, u32[]{:S(2)}) collective-permute-start(bf16[128,1024]{1,0:T(8,128)(2,1)S(1)} %get-tuple-element.95), channel_id=1, source_target_pairs={{0,8},{1,9},{2,10},{3,11},{4,12},{5,13},{6,14},{7,15},{8,0},{9,1},... | collective-permute-start | bytes 786440 | tf_op jit(solution)/shard_map/ppermute | solution.py:686
  566.5 12.7 %collective-permute-start.47 = (bf16[128,1024]{1,0:T(8,128)(2,1)S(1)}, bf16[128,1024]{1,0:T(8,128)(2,1)S(1)}, u32[]{:S(2)}, u32[]{:S(2)}) collective-permute-start(bf16[128,1024]{1,0:T(8,128)(2,1)S(1)} %get-tuple-element.94), channel_id=1, source_target_pairs={{0,4},{1,5},{2,6},{3,7},{4,8},{5,9},{6,10},{7,11},{8,12},{9,13},{1... | collective-permute-start | bytes 786440 | tf_op jit(solution)/shard_map/ppermute | solution.py:686
  570.8 9.8 %collective-permute-start.51 = (bf16[88,1024]{1,0:T(8,128)(2,1)}, bf16[88,1024]{1,0:T(8,128)(2,1)S(1)}, u32[]{:S(2)}, u32[]{:S(2)}) collective-permute-start(bf16[88,1024]{1,0:T(8,128)(2,1)} %reduce-scatter.5.cloned.1.call-done), channel_id=1, source_target_pairs={{0,16},{16,0},{1,17},{17,1},{2,18},{18,2},{3,19},{19,3},{4,20},{20... | collective-permute-start | bytes 540680 | tf_op jit(solution)/shard_map/ppermute | solution.py:607
  579.4 7.3 %collective-permute-start.48 = (bf16[128,1024]{1,0:T(8,128)(2,1)S(1)}, bf16[128,1024]{1,0:T(8,128)(2,1)S(1)}, u32[]{:S(2)}, u32[]{:S(2)}) collective-permute-start(bf16[128,1024]{1,0:T(8,128)(2,1)S(1)} %fusion.40), channel_id=1, source_target_pairs={{0,16},{16,0},{1,17},{17,1},{2,18},{18,2},{3,19},{19,3},{4,20},{20... | collective-permute-start | bytes 786440 | tf_op jit(solution)/shard_map/ppermute | solution.py:607
  584.1 6.4 %collective-permute-start.50 = (bf16[64,16,88]{2,1,0:T(8,128)(2,1)S(1)}, bf16[64,16,88]{2,1,0:T(8,128)(2,1)S(1)}, u32[]{:S(2)}, u32[]{:S(2)}) collective-permute-start(bf16[64,16,88]{2,1,0:T(8,128)(2,1)S(1)} %reshape.274), channel_id=1, source_target_pairs={{0,16},{16,0},{1,17},{17,1},{2,18},{18,2},{3,19},{19,3},{4,20},{20... | collective-permute-start | bytes 540680 | tf_op jit(solution)/shard_map/ppermute | solution.py:607
  585.5 7.8 %collective-permute-start.49 = (bf16[64,16,88]{2,1,0:T(8,128)(2,1)S(1)}, bf16[64,16,88]{2,1,0:T(8,128)(2,1)S(1)}, u32[]{:S(2)}, u32[]{:S(2)}) collective-permute-start(bf16[64,16,88]{2,1,0:T(8,128)(2,1)S(1)} %reshape.273), channel_id=1, source_target_pairs={{0,16},{16,0},{1,17},{17,1},{2,18},{18,2},{3,19},{19,3},{4,20},{20... | collective-permute-start | bytes 540680 | tf_op jit(solution)/shard_map/ppermute | solution.py:607
  (52 other events, 597.1 us)
Sparse Core Ops, SparseCore 0:
  13.4 64.4 all-gather.2
  80.8 102.0 all-gather.4
  267.3 63.3 reduce-scatter.4
  346.6 82.0 reduce-scatter.2
